TPU v7x, 768 devices: a whole 4x8x12 slice. The times are simulated.
768 devices in a mesh: dom: 12 (over z), grp: 64 (over y, x, core).
Axes of the slice: x: 4, y: 8, z: 12, core: 2. Of those that a mesh axis runs over, the one named last changes fastest.
Arguments:
- positions: float32 [3, 1572864], P(None, ('dom', 'grp')), may hold values from -6 to 6
- velocities: float32 [3, 1572864], P(None, ('dom', 'grp')), may hold values from -6 to 6
- masses: float32 [1572864], P(('dom', 'grp')), may hold values from 1 to 16
- atom_kinds: int32 [1572864], P(('dom', 'grp')), may hold values from 0 to 99
- frag_atoms: int32 [24576, 64], P(('dom', 'grp')), may hold values from -1 to 2175, as said below
- assign: int32 [2, 24576], P(None, ('dom', 'grp')), may hold values from -1 to 63, as said below
- embed_table: bfloat16 [100, 256], replicated, may hold values from -8 to 8
- neigh_table: bfloat16 [100, 256], replicated, may hold values from -2 to 2
- w_query: bfloat16 [256, 256], replicated, may hold values from -0.375 to 0.375
- w_key: bfloat16 [256, 256], replicated, may hold values from -0.375 to 0.375
- w_value: bfloat16 [256, 256], replicated, may hold values from -0.375 to 0.375
- w_energy: float32 [256], replicated, may hold values from -0.375 to 0.375
- w_force: float32 [256, 8], replicated, may hold values from -0.375 to 0.375
- head_decay: float32 [8], replicated, may hold values from 0.05 to 1
Outputs:
- positions_out: float32 [3, 1572864], P(None, ('dom', 'grp'))
- velocities_out: float32 [3, 1572864], P(None, ('dom', 'grp'))
- energies: float32 [2, 24576], P(None, ('dom', 'grp'))
Inputs may be any that keep to these rules, and one draw needn't show every extreme that they name: `frag_atoms`: entries -1 mark padding; a slot's live indices come first and run consecutively. Slots that are not active in a step have no live indices. `assign`: the active slots are the same in every step. Among the slots of one device, at most 2 name the same grp index in a step, and among the devices of one dom index at most 16 slots name the same grp index in a step.
All inputs are finite; a program needn't handle non-finite values.
Results may differ from a plain program's by a relative error of at most 0.0076.
Values sent between devices are 32-bit elements; how exact they have to be, the bound alone decides.
A program may use at most 32 MiB of HBM per device.

v0:
```python
import math

import jax
import jax.numpy as jnp
from jax import lax
from jax.sharding import PartitionSpec as P

HALO = 64
STEPS = 2
RECV = 16


TIME_STEP = 0.05
NEAR_RATE = 0.5
HIGHEST_MODE = lax.Precision.HIGHEST


def padded(block, sides, width):
    for axis, dim in sides:
        count = lax.axis_size(axis)
        forward = [(i, i + 1) for i in range(count - 1)]
        forward.append((count - 1, 0))
        backward = [(target, source) for source, target in forward]
        low = lax.ppermute(
            lax.slice_in_dim(block, block.shape[dim] - width, None, axis=dim), axis, forward
        )
        high = lax.ppermute(lax.slice_in_dim(block, 0, width, axis=dim), axis, backward)
        block = jnp.concatenate([low, block, high], axis=dim)
    return block


def passed_along(block, axis, distance):
    devices = range(lax.axis_size(axis))
    route = [((i - distance) % len(devices), i) for i in devices]
    return lax.ppermute(block, axis, route)


def fragment_model(
    coords, kinds, embed_table, neigh_table, w_query, w_key, w_value, w_energy, w_force, head_decay
):
    frag_count, atom_count = kinds.shape
    model_width = w_query.shape[0]
    head_count = head_decay.shape[0]
    head_width = model_width // head_count
    atom_mask = (kinds >= 0).astype(jnp.float32)
    pair_mask = atom_mask[:, :, None] * atom_mask[:, None, :]
    squared = jnp.zeros((frag_count, atom_count, atom_count), jnp.float32)
    for component in range(3):
        column = coords[:, component, :]
        spread = column[:, :, None] - column[:, None, :]
        squared = squared + spread * spread
    kind_ids = jnp.arange(embed_table.shape[0]).astype(jnp.float32)
    one_hot = (kinds[:, :, None] == kind_ids[None, None, :]).astype(jnp.float32)
    others = 1.0 - jnp.eye(atom_count, dtype=jnp.float32)
    nearby = jnp.exp(-NEAR_RATE * squared) * pair_mask * others[None]
    tallies = jnp.einsum("fij,fjt->fit", nearby, one_hot, precision=HIGHEST_MODE)
    summed = jnp.einsum(
        "fit,tc->fic", one_hot, embed_table.astype(jnp.float32), precision=HIGHEST_MODE
    )
    summed = summed + jnp.einsum(
        "fit,tc->fic", tallies, neigh_table.astype(jnp.float32), precision=HIGHEST_MODE
    )
    hidden = (jax.nn.silu(summed) * atom_mask[:, :, None]).astype(jnp.bfloat16)
    row_block = hidden.reshape(frag_count * atom_count, model_width)
    split_shape = (frag_count, atom_count, head_count, head_width)
    query_rows = (
        jnp.dot(row_block, w_query, preferred_element_type=jnp.float32)
        .astype(jnp.bfloat16)
        .reshape(split_shape)
    )
    key_rows = (
        jnp.dot(row_block, w_key, preferred_element_type=jnp.float32)
        .astype(jnp.bfloat16)
        .reshape(split_shape)
    )
    value_rows = (
        jnp.dot(row_block, w_value, preferred_element_type=jnp.float32)
        .astype(jnp.bfloat16)
        .reshape(split_shape)
    )
    scores = jnp.einsum(
        "fihd,fjhd->fhij", query_rows, key_rows, preferred_element_type=jnp.float32
    ) / math.sqrt(head_width)
    envelope = jnp.exp(-head_decay[None, :, None, None] * squared[:, None, :, :])
    weights = jax.nn.silu(scores) * envelope * pair_mask[:, None, :, :]
    rounded = weights.astype(jnp.bfloat16)
    mixture = jnp.einsum("fhij,fjhd->fihd", rounded, value_rows, preferred_element_type=jnp.float32)
    updated = hidden.astype(jnp.float32) + mixture.reshape(frag_count, atom_count, model_width)
    flat_state = updated.reshape(frag_count * atom_count, model_width)
    atom_energy = (
        jnp.dot(flat_state, w_energy, precision=HIGHEST_MODE).reshape(frag_count, atom_count)
        * atom_mask
    )
    scalars = jnp.dot(flat_state, w_force, precision=HIGHEST_MODE).reshape(
        frag_count, atom_count, head_count
    )
    coupling = jnp.einsum("fhij,fjh->fij", weights, scalars, precision=HIGHEST_MODE)
    row_total = jnp.sum(coupling, axis=2)
    pulled = jnp.einsum("fij,fcj->fci", coupling, coords, precision=HIGHEST_MODE)
    forces = (coords * row_total[:, None, :] - pulled) * atom_mask[:, None, :]
    return (forces, atom_energy)


def body(
    positions,
    velocities,
    masses,
    atom_kinds,
    frag_atoms,
    assign,
    embed_table,
    neigh_table,
    w_query,
    w_key,
    w_value,
    w_energy,
    w_force,
    head_decay,
):
    atom_local = positions.shape[1]
    frag_slots, frag_width = frag_atoms.shape
    group_size = lax.axis_size("grp")
    slot_cap = max(2, 2 * RECV // group_size)
    slot_total = group_size * slot_cap
    row_width = 4 * frag_width
    ext_width = atom_local + 2 * HALO
    index_flat = frag_atoms.reshape(-1)
    real_atom = index_flat >= 0
    safe_index = jnp.maximum(index_flat, 0)
    seg_ids = jnp.where(real_atom, safe_index, ext_width)
    kinds_float = atom_kinds.astype(jnp.float32)[None, :]
    empty_row = jnp.concatenate(
        [jnp.zeros((3 * frag_width,), jnp.float32), -jnp.ones((frag_width,), jnp.float32)]
    )

    def evaluate_block(row_block):
        shaped = row_block.reshape(row_block.shape[0], 4, frag_width)
        forces, atom_energy = fragment_model(
            shaped[:, :3],
            shaped[:, 3],
            embed_table,
            neigh_table,
            w_query,
            w_key,
            w_value,
            w_energy,
            w_force,
            head_decay,
        )
        return jnp.concatenate([forces, atom_energy[:, None, :]], axis=1).reshape(
            row_block.shape[0], row_width
        )

    energies = []
    kinds_base = None
    for md_step in range(STEPS):
        if md_step == 0:
            outgoing = jnp.concatenate([positions, kinds_float], axis=0)
        else:
            outgoing = positions
        extended = padded(outgoing, (("dom", 1),), HALO)
        if md_step == 0:
            kinds_base = jnp.where(real_atom, extended[3][safe_index], -1.0)
        receiver = assign[md_step]
        active = receiver >= 0
        frag_kinds = jnp.where(jnp.repeat(active, frag_width), kinds_base, -1.0).reshape(
            frag_slots, frag_width
        )
        frag_pos = extended[:3][:, safe_index].reshape(3, frag_slots, frag_width).transpose(1, 0, 2)
        payload = jnp.concatenate([frag_pos, frag_kinds[:, None, :]], axis=1).reshape(
            frag_slots, row_width
        )
        slot_ids = jnp.arange(frag_slots, dtype=jnp.int32)
        earlier = (receiver[:, None] == receiver[None, :]) & (slot_ids[None, :] < slot_ids[:, None])
        order_in = jnp.sum(earlier.astype(jnp.int32), axis=1)
        target = jnp.where(active, receiver * slot_cap + order_in, slot_total)
        outbox = (
            jnp.broadcast_to(empty_row[None, :], (slot_total, row_width))
            .at[target]
            .set(payload, mode="drop")
        )
        arrived = lax.all_to_all(
            outbox.reshape(group_size, slot_cap, row_width),
            "grp",
            split_axis=0,
            concat_axis=0,
            tiled=True,
        ).reshape(slot_total, row_width)
        occupied = jnp.max(arrived[:, 3 * frag_width :], axis=1) >= 0
        position_rank = jnp.cumsum(occupied.astype(jnp.int32)) - 1
        chosen = (
            jnp.zeros((RECV,), jnp.int32)
            .at[jnp.where(occupied, position_rank, RECV)]
            .set(jnp.arange(slot_total, dtype=jnp.int32), mode="drop")
        )
        filled = jnp.arange(RECV, dtype=jnp.int32) < jnp.sum(occupied.astype(jnp.int32))
        workload = jnp.where(filled[:, None], arrived[chosen], empty_row[None, :])
        row_count = workload.shape[0]
        block_rows = math.gcd(row_count, 16)
        grouped = workload.reshape(row_count // block_rows, block_rows, row_width)
        computed = lax.map(evaluate_block, grouped).reshape(row_count, row_width)
        replies = (
            jnp.zeros((slot_total, row_width), jnp.float32)
            .at[jnp.where(filled, chosen, slot_total)]
            .set(computed, mode="drop")
        )
        answer = lax.all_to_all(
            replies.reshape(group_size, slot_cap, row_width),
            "grp",
            split_axis=0,
            concat_axis=0,
            tiled=True,
        ).reshape(slot_total, row_width)
        results = jnp.where(active[:, None], answer[jnp.minimum(target, slot_total - 1)], 0.0)
        shaped = results.reshape(frag_slots, 4, frag_width)
        energies.append(jnp.sum(shaped[:, 3], axis=1))
        force_rows = shaped[:, :3].transpose(1, 0, 2).reshape(3, frag_slots * frag_width)
        force_ext = jax.ops.segment_sum(force_rows.T, seg_ids, num_segments=ext_width + 1)[
            :ext_width
        ].T
        from_upper = passed_along(force_ext[:, :HALO], "dom", -1)
        from_lower = passed_along(force_ext[:, HALO + atom_local :], "dom", 1)
        summed_force = force_ext[:, HALO : HALO + atom_local]
        summed_force = (
            summed_force.at[:, :HALO].add(from_lower).at[:, atom_local - HALO :].add(from_upper)
        )
        velocities = velocities + TIME_STEP * summed_force / masses[None, :]
        positions = positions + TIME_STEP * velocities
    return (positions, velocities, jnp.stack(energies))


def solution(mesh):
    return jax.shard_map(
        body,
        mesh=mesh,
        in_specs=(
            P(None, ("dom", "grp")),
            P(None, ("dom", "grp")),
            P(("dom", "grp")),
            P(("dom", "grp")),
            P(("dom", "grp"), None),
            P(None, ("dom", "grp")),
            P(),
            P(),
            P(),
            P(),
            P(),
            P(),
            P(),
            P(),
        ),
        out_specs=(P(None, ("dom", "grp")), P(None, ("dom", "grp")), P(None, ("dom", "grp"))),
        check_vma=False,
    )
```

profile of v0, /device:TPU:1, one launch (start us, length us, event | category | flops | bytes accessed | tf_op | source)
XLA Modules:
  0.0 250.2 jit_solution(5987691922700982727)
XLA Ops:
  2.2 4.8 %collective-permute-start = (f32[4,64]{1,0:T(4,128)S(1)}, f32[4,64]{1,0:T(4,128)S(1)}, u32[]{:S(2)}, u32[]{:S(2)}) collective-permute-start(f32[4,64]{1,0:T(4,128)S(1)} %get-tuple-element.142), channel_id=1, source_target_pairs={{0,64},{64,128},{128,192},{192,256},{256,320},{320,384},{384,448},... | collective-permute-start | bytes 3080 | tf_op jit(solution)/shard_map/ppermute | solution.py:24
  7.0 12.2 %collective-permute-start.1 = (f32[4,64]{1,0:T(4,128)S(1)}, f32[4,64]{1,0:T(4,128)S(1)}, u32[]{:S(2)}, u32[]{:S(2)}) collective-permute-start(f32[4,64]{1,0:T(4,128)S(1)} %get-tuple-element.141), channel_id=1, source_target_pairs={{64,0},{128,64},{192,128},{256,192},{320,256},{384,320},{448,384},... | collective-permute-start | bytes 3080 | tf_op jit(solution)/shard_map/ppermute | solution.py:27
  24.0 11.8 %gather_fusion.1 = f32[2048]{0:T(1024)S(1)} fusion(f32[2176]{0:T(1024)S(1)} %slice_reduce_fusion.4, s32[2048]{0:T(1024)S(1)} %broadcast_clamp_fusion), kind=kCustom, calls=%fused_computation.1 | custom fusion | bytes 24576 | tf_op jit(solution)/shard_map/gather | solution.py:163
  36.3 5.5 %gather_fusion = f32[2048,3]{1,0:T(8,128)S(1)} fusion(f32[3,2176]{0,1:T(8,128)S(1)} %copy.163, s32[2048]{0:T(1024)S(1)} %broadcast_clamp_fusion), kind=kCustom, calls=%fused_computation | custom fusion | bytes 57344 | tf_op jit(solution)/shard_map/gather | solution.py:169
  44.7 11.1 %all-to-all-start = ((f32[64,2,256]{2,1,0:T(2,128)}), f32[64,2,256]{2,1,0:T(2,128)S(1)}, u32[]{:S(2)}, u32[]{:S(2)}) async-start(f32[64,2,256]{2,1,0:T(2,128)} %reshape.589), calls=%async_computation | async-start | bytes 262144 | tf_op jit(solution)/shard_map/all_to_all | solution.py:182
  56.3 10.6 %all-to-all-done = f32[64,2,256]{2,1,0:T(2,128)S(1)} async-done(((f32[64,2,256]{2,1,0:T(2,128)}), f32[64,2,256]{2,1,0:T(2,128)S(1)}, u32[]{:S(2)}, u32[]{:S(2)}) %all-to-all-start) | async-done | bytes 131104 | tf_op jit(solution)/shard_map/all_to_all | solution.py:182
  81.9 3.7 %multiply_multiply_fusion.1 = f32[16,8,64,64]{3,2,1,0:T(8,128)S(1)} fusion(f32[16,64,64]{2,1,0:T(8,128)} %broadcast_multiply_fusion.1, f32[16,64,64]{2,1,0:T(8,128)} %multiply_add_fusion.1, f32[8]{0:T(128)} %neg.27, bf16[16,64,8,32]{1,0,3,2:T(8,128)(2,1)S(1)} %reshape.594, bf16[16,64,8,32]{1,0,3,2:T(8,128)(2,1)} %reshape.593), kind=kOutput, calls=%fused_computation.18 | convolution fusion | flops 37748736 | bytes 3670048 | tf_op jit(solution)/shard_map/while/body/eval_jaxpr/fihd,fjhd->fhij/dot_general | solution.py:81
  87.6 2.6 %fusion.2 = f32[16,8,32,64]{3,2,1,0:T(8,128)} fusion(f32[16,8,64,64]{3,2,1,0:T(8,128)S(1)} %multiply_multiply_fusion.1, bf16[16,64,8,32]{1,0,3,2:T(8,128)(2,1)S(1)} %reshape.592), kind=kOutput, calls=%fused_computation.21 | convolution fusion | flops 34078720 | bytes 3670016 | tf_op jit(solution)/shard_map/while/body/eval_jaxpr/fhij,fjhd->fihd/dot_general | solution.py:87
  90.1 2.2 copy.176
  95.2 3.0 %multiply_reduce_fusion.1 = f32[16,64,64]{1,2,0:T(8,128)S(1)} fusion(f32[16,8,64,64]{3,2,1,0:T(8,128)} %copy-done.2, f32[16,64,8]{1,2,0:T(8,128)S(1)} %fusion.12), kind=kLoop, calls=%fused_computation.16 | loop fusion | flops 983040 | bytes 2392064 | tf_op jit(solution)/shard_map/while/body/eval_jaxpr/fhij,fjh->fij/dot_general | solution.py:97
  101.6 4.6 %all-to-all-start.1 = ((f32[64,2,256]{2,1,0:T(2,128)}), f32[64,2,256]{2,1,0:T(2,128)S(1)}, u32[]{:S(2)}, u32[]{:S(2)}) async-start(f32[64,2,256]{2,1,0:T(2,128)} %reshape.597), calls=%async_computation.1 | async-start | bytes 262144 | tf_op jit(solution)/shard_map/all_to_all | solution.py:207
  106.3 11.2 %all-to-all-done.1 = f32[64,2,256]{2,1,0:T(2,128)S(1)} async-done(((f32[64,2,256]{2,1,0:T(2,128)}), f32[64,2,256]{2,1,0:T(2,128)S(1)}, u32[]{:S(2)}, u32[]{:S(2)}) %all-to-all-start.1) | async-done | bytes 131104 | tf_op jit(solution)/shard_map/all_to_all | solution.py:207
  119.5 13.8 %scatter_custom_fusion.3 = f32[2177,3]{1,0:T(8,128)S(1)} fusion(s32[2048]{0:T(1024)S(1)} %reshape.697, f32[2048,3]{1,0:T(8,128)S(1)} %bitcast.179, f32[]{:T(128)} %constant.169.clone.1), kind=kCustom, calls=%fused_computation.55 | custom fusion | flops 6144 | bytes 26128 | tf_op jit(solution)/shard_map/scatter-add | solution.py:218
  136.5 4.6 %collective-permute-start.3 = (f32[3,64]{1,0:T(4,128)S(1)}, f32[3,64]{1,0:T(4,128)S(1)}, u32[]{:S(2)}, u32[]{:S(2)}) collective-permute-start(f32[3,64]{1,0:T(4,128)S(1)} %get-tuple-element.145), channel_id=1, source_target_pairs={{64,0},{128,64},{192,128},{256,192},{320,256},{384,320},{448,384},... | collective-permute-start | bytes 2312 | tf_op jit(solution)/shard_map/ppermute | solution.py:35
  144.3 4.9 %collective-permute-start.5 = (f32[3,64]{1,0:T(4,128)S(1)}, f32[3,64]{1,0:T(4,128)S(1)}, u32[]{:S(2)}, u32[]{:S(2)}) collective-permute-start(f32[3,64]{1,0:T(4,128)S(1)} %get-tuple-element.151), channel_id=1, source_target_pairs={{64,0},{128,64},{192,128},{256,192},{320,256},{384,320},{448,384},... | collective-permute-start | bytes 2312 | tf_op jit(solution)/shard_map/ppermute | solution.py:27
  150.4 5.5 %gather_fusion.4 = f32[2048,3]{1,0:T(8,128)S(1)} fusion(f32[3,2176]{0,1:T(8,128)S(1)} %copy.179, s32[2048]{0:T(1024)S(1)} %copy-done.20), kind=kCustom, calls=%fused_computation.4 | custom fusion | bytes 57344 | tf_op jit(solution)/shard_map/gather | solution.py:169
  157.4 17.0 %all_to_all.20 = f32[64,2,256]{2,1,0:T(2,128)S(1)} all-to-all(f32[64,2,256]{2,1,0:T(2,128)S(1)} %reshape.602), channel_id=1, replica_groups=mesh['dom'=12,'grp'=64] {'grp'}, dimensions={0} | all-to-all | bytes 262144 | tf_op jit(solution)/shard_map/all_to_all | solution.py:182
  189.4 3.7 %multiply_multiply_fusion = f32[16,8,64,64]{3,2,1,0:T(8,128)S(1)} fusion(f32[16,64,64]{2,1,0:T(8,128)} %broadcast_multiply_fusion, f32[16,64,64]{2,1,0:T(8,128)} %multiply_add_fusion, f32[8]{0:T(128)S(1)} %copy-done.50, bf16[16,64,8,32]{1,0,3,2:T(8,128)(2,1)S(1)} %reshape.607, bf16[16,64,8,32]{1,0,3,2:T(8,128)(2,1)} %reshape.606), kind=kOutput, calls=%fused_computation.17 | convolution fusion | flops 37748736 | bytes 3670048 | tf_op jit(solution)/shard_map/while/body/eval_jaxpr/fihd,fjhd->fhij/dot_general | solution.py:81
  195.0 2.6 %fusion = f32[16,8,32,64]{3,2,1,0:T(8,128)} fusion(f32[16,8,64,64]{3,2,1,0:T(8,128)S(1)} %multiply_multiply_fusion, bf16[16,64,8,32]{1,0,3,2:T(8,128)(2,1)S(1)} %reshape.605), kind=kOutput, calls=%fused_computation.19 | convolution fusion | flops 34078720 | bytes 3670016 | tf_op jit(solution)/shard_map/while/body/eval_jaxpr/fhij,fjhd->fihd/dot_general | solution.py:87
  202.6 3.0 %multiply_reduce_fusion = f32[16,64,64]{1,2,0:T(8,128)S(1)} fusion(f32[16,8,64,64]{3,2,1,0:T(8,128)} %copy-done.1, f32[16,64,8]{1,2,0:T(8,128)S(1)} %fusion.14), kind=kLoop, calls=%fused_computation.15 | loop fusion | flops 983040 | bytes 2392064 | tf_op jit(solution)/shard_map/while/body/eval_jaxpr/fhij,fjh->fij/dot_general | solution.py:97
  208.5 4.7 %all-to-all-start.3 = ((f32[64,2,256]{2,1,0:T(2,128)}), f32[64,2,256]{2,1,0:T(2,128)S(1)}, u32[]{:S(2)}, u32[]{:S(2)}) async-start(f32[64,2,256]{2,1,0:T(2,128)} %reshape.610), calls=%async_computation.3 | async-start | bytes 262144 | tf_op jit(solution)/shard_map/all_to_all | solution.py:207
  214.4 10.2 %all-to-all-done.3 = f32[64,2,256]{2,1,0:T(2,128)S(1)} async-done(((f32[64,2,256]{2,1,0:T(2,128)}), f32[64,2,256]{2,1,0:T(2,128)S(1)}, u32[]{:S(2)}, u32[]{:S(2)}) %all-to-all-start.3) | async-done | bytes 131104 | tf_op jit(solution)/shard_map/all_to_all | solution.py:207
  226.2 13.8 %scatter_custom_fusion.7 = f32[2177,3]{1,0:T(8,128)S(1)} fusion(s32[2048]{0:T(1024)S(1)} %reshape.697, f32[2048,3]{1,0:T(8,128)S(1)} %bitcast.178, f32[]{:T(128)} %constant.169.clone.1), kind=kCustom, calls=%fused_computation.53 | custom fusion | flops 6144 | bytes 26128 | tf_op jit(solution)/shard_map/scatter-add | solution.py:218
  242.4 5.1 %collective-permute-start.7 = (f32[3,64]{1,0:T(4,128)S(1)}, f32[3,64]{1,0:T(4,128)S(1)}, u32[]{:S(2)}, u32[]{:S(2)}) collective-permute-start(f32[3,64]{1,0:T(4,128)S(1)} %get-tuple-element.143), channel_id=1, source_target_pairs={{64,0},{128,64},{192,128},{256,192},{320,256},{384,320},{448,384},... | collective-permute-start | bytes 2312 | tf_op jit(solution)/shard_map/ppermute | solution.py:35
  (282 shorter events, 76.1 us)
Async XLA Ops:
  0.6 76.8 %copy-start = (bf16[256,256]{1,0:T(8,128)(2,1)S(1)}, bf16[256,256]{1,0:T(8,128)(2,1)}, u32[]{:S(2)}) copy-start(bf16[256,256]{1,0:T(8,128)(2,1)} %param.31) | copy-start | bytes 393220
  2.2 21.7 %collective-permute-start = (f32[4,64]{1,0:T(4,128)S(1)}, f32[4,64]{1,0:T(4,128)S(1)}, u32[]{:S(2)}, u32[]{:S(2)}) collective-permute-start(f32[4,64]{1,0:T(4,128)S(1)} %get-tuple-element.142), channel_id=1, source_target_pairs={{0,64},{64,128},{128,192},{192,256},{256,320},{320,384},{384,448},... | collective-permute-start | bytes 3080 | tf_op jit(solution)/shard_map/ppermute | solution.py:24
  7.0 16.9 %collective-permute-start.1 = (f32[4,64]{1,0:T(4,128)S(1)}, f32[4,64]{1,0:T(4,128)S(1)}, u32[]{:S(2)}, u32[]{:S(2)}) collective-permute-start(f32[4,64]{1,0:T(4,128)S(1)} %get-tuple-element.141), channel_id=1, source_target_pairs={{64,0},{128,64},{192,128},{256,192},{320,256},{384,320},{448,384},... | collective-permute-start | bytes 3080 | tf_op jit(solution)/shard_map/ppermute | solution.py:27
  44.7 22.2 %all-to-all-start = ((f32[64,2,256]{2,1,0:T(2,128)}), f32[64,2,256]{2,1,0:T(2,128)S(1)}, u32[]{:S(2)}, u32[]{:S(2)}) async-start(f32[64,2,256]{2,1,0:T(2,128)} %reshape.589), calls=%async_computation | async-start | bytes 262144 | tf_op jit(solution)/shard_map/all_to_all | solution.py:182
  98.2 44.0 %copy-start.13 = (f32[3,2048]{1,0:T(4,128)S(1)}, f32[3,2048]{1,0:T(4,128)}, u32[]{:S(2)}) copy-start(f32[3,2048]{1,0:T(4,128)} %param.22) | copy-start | bytes 73732
  98.2 44.0 %copy-start.17 = (f32[3,2048]{1,0:T(4,128)S(1)}, f32[3,2048]{1,0:T(4,128)}, u32[]{:S(2)}) copy-start(f32[3,2048]{1,0:T(4,128)} %param.23) | copy-start | bytes 73732
  98.2 44.0 %copy-start.28 = (f32[2048]{0:T(1024)S(1)}, f32[2048]{0:T(1024)}, u32[]{:S(2)}) copy-start(f32[2048]{0:T(1024)} %param.24) | copy-start | bytes 24580
  98.5 50.7 %copy-start.46 = (s32[32,1]{0,1:T(1,128)S(1)}, s32[32,1]{0,1:T(1,128)}, u32[]{:S(2)}) copy-start(s32[32,1]{0,1:T(1,128)} %get-tuple-element.132) | copy-start | bytes 388
  101.6 48.8 %copy-start.20 = (s32[2048]{0:T(1024)S(1)}, s32[2048]{0:T(1024)}, u32[]{:S(2)}) copy-start(s32[2048]{0:T(1024)} %copy-done.19) | copy-start | bytes 24580
  101.6 15.9 %all-to-all-start.1 = ((f32[64,2,256]{2,1,0:T(2,128)}), f32[64,2,256]{2,1,0:T(2,128)S(1)}, u32[]{:S(2)}, u32[]{:S(2)}) async-start(f32[64,2,256]{2,1,0:T(2,128)} %reshape.597), calls=%async_computation.1 | async-start | bytes 262144 | tf_op jit(solution)/shard_map/all_to_all | solution.py:207
  133.3 46.4 %copy-start.33 = (f32[4,64]{1,0:T(4,128)S(1)}, f32[4,64]{1,0:T(4,128)}, u32[]{:S(2)}) copy-start(f32[4,64]{1,0:T(4,128)} %constant.179.clone.1) | copy-start | bytes 3076
  133.4 49.3 %copy-start.31 = (f32[64,64]{1,0:T(8,128)S(1)}, f32[64,64]{1,0:T(8,128)}, u32[]{:S(2)}) copy-start(f32[64,64]{1,0:T(8,128)} %copy-done.30) | copy-start | bytes 49156
  133.4 49.3 %copy-start.52 = (f32[100]{0:T(128)S(1)}, f32[100]{0:T(128)}, u32[]{:S(2)}) copy-start(f32[100]{0:T(128)} %copy-done.51) | copy-start | bytes 1204
  133.8 7.3 %collective-permute-start.2 = (f32[3,64]{1,0:T(4,128)S(1)}, f32[3,64]{1,0:T(4,128)S(1)}, u32[]{:S(2)}, u32[]{:S(2)}) collective-permute-start(f32[3,64]{1,0:T(4,128)S(1)} %get-tuple-element.146), channel_id=1, source_target_pairs={{704,0},{0,64},{64,128},{128,192},{192,256},{256,320},{320,384},{3... | collective-permute-start | bytes 2312 | tf_op jit(solution)/shard_map/ppermute | solution.py:35
  136.5 5.4 %collective-permute-start.3 = (f32[3,64]{1,0:T(4,128)S(1)}, f32[3,64]{1,0:T(4,128)S(1)}, u32[]{:S(2)}, u32[]{:S(2)}) collective-permute-start(f32[3,64]{1,0:T(4,128)S(1)} %get-tuple-element.145), channel_id=1, source_target_pairs={{64,0},{128,64},{192,128},{256,192},{320,256},{384,320},{448,384},... | collective-permute-start | bytes 2312 | tf_op jit(solution)/shard_map/ppermute | solution.py:35
  142.4 6.8 %collective-permute-start.4 = (f32[3,64]{1,0:T(4,128)S(1)}, f32[3,64]{1,0:T(4,128)S(1)}, u32[]{:S(2)}, u32[]{:S(2)}) collective-permute-start(f32[3,64]{1,0:T(4,128)S(1)} %get-tuple-element.152), channel_id=1, source_target_pairs={{0,64},{64,128},{128,192},{192,256},{256,320},{320,384},{384,448},... | collective-permute-start | bytes 2312 | tf_op jit(solution)/shard_map/ppermute | solution.py:24
  144.3 5.6 %collective-permute-start.5 = (f32[3,64]{1,0:T(4,128)S(1)}, f32[3,64]{1,0:T(4,128)S(1)}, u32[]{:S(2)}, u32[]{:S(2)}) collective-permute-start(f32[3,64]{1,0:T(4,128)S(1)} %get-tuple-element.151), channel_id=1, source_target_pairs={{64,0},{128,64},{192,128},{256,192},{320,256},{384,320},{448,384},... | collective-permute-start | bytes 2312 | tf_op jit(solution)/shard_map/ppermute | solution.py:27
  205.8 43.5 %copy-start.10 = (f32[3,2048]{1,0:T(4,128)S(1)}, f32[3,2048]{1,0:T(4,128)}, u32[]{:S(2)}) copy-start(f32[3,2048]{1,0:T(4,128)} %copy-done.9) | copy-start | bytes 73732
  205.8 43.5 %copy-start.12 = (f32[3,2048]{1,0:T(4,128)S(1)}, f32[3,2048]{1,0:T(4,128)}, u32[]{:S(2)}) copy-start(f32[3,2048]{1,0:T(4,128)} %copy-done.11) | copy-start | bytes 73732
  205.8 43.5 %copy-start.18 = (f32[3,2048]{1,0:T(4,128)S(1)}, f32[3,2048]{1,0:T(4,128)}, u32[]{:S(2)}) copy-start(f32[3,2048]{1,0:T(4,128)} %param.23) | copy-start | bytes 73732
  205.8 43.5 %copy-start.29 = (f32[2048]{0:T(1024)S(1)}, f32[2048]{0:T(1024)}, u32[]{:S(2)}) copy-start(f32[2048]{0:T(1024)} %param.24) | copy-start | bytes 24580
  208.5 16.0 %all-to-all-start.3 = ((f32[64,2,256]{2,1,0:T(2,128)}), f32[64,2,256]{2,1,0:T(2,128)S(1)}, u32[]{:S(2)}, u32[]{:S(2)}) async-start(f32[64,2,256]{2,1,0:T(2,128)} %reshape.610), calls=%async_computation.3 | async-start | bytes 262144 | tf_op jit(solution)/shard_map/all_to_all | solution.py:207
  240.5 7.7 %collective-permute-start.6 = (f32[3,64]{1,0:T(4,128)S(1)}, f32[3,64]{1,0:T(4,128)S(1)}, u32[]{:S(2)}, u32[]{:S(2)}) collective-permute-start(f32[3,64]{1,0:T(4,128)S(1)} %get-tuple-element.144), channel_id=1, source_target_pairs={{704,0},{0,64},{64,128},{128,192},{192,256},{256,320},{320,384},{3... | collective-permute-start | bytes 2312 | tf_op jit(solution)/shard_map/ppermute | solution.py:35
  242.4 6.6 %collective-permute-start.7 = (f32[3,64]{1,0:T(4,128)S(1)}, f32[3,64]{1,0:T(4,128)S(1)}, u32[]{:S(2)}, u32[]{:S(2)}) collective-permute-start(f32[3,64]{1,0:T(4,128)S(1)} %get-tuple-element.143), channel_id=1, source_target_pairs={{64,0},{128,64},{192,128},{256,192},{320,256},{384,320},{448,384},... | collective-permute-start | bytes 2312 | tf_op jit(solution)/shard_map/ppermute | solution.py:35
  (42 other events, 623.0 us)
where the time goes:
time: 255 us; the launch traced here: 250 us
  other arithmetic  58 us (23%)
  starting transfers between devices  57.7 us (23%)
  local copies, waits for them, and re-layouts  56.8 us (22%)
  waiting for transfers between devices  32.6 us (13%)
  matrix products  25.8 us (10%)
  blocking collectives  17 us (7%)
    scatter-add x2, other arithmetic, body(): jax.ops.segment_sum(force_rows.T, seg_ids, num_segments=ext_width + 1)  27.6 us
    all_to_all x2, waiting for transfers between devices, body(): lax.all_to_all(replies.reshape(group_size, slot_cap, row_width), 'grp', s...  21.4 us
    ppermute x2, starting transfers between devices, padded(): lax.ppermute(lax.slice_in_dim(block, 0, width, axis=dim), axis, backward)  17.1 us
    all_to_all x1, blocking collectives, body(): lax.all_to_all(outbox.reshape(group_size, slot_cap, row_width), 'grp', sp...  17 us
    ppermute x4, starting transfers between devices, passed_along(): return lax.ppermute(block, axis, route)  13.5 us
    gather x2, local copies, waits for them, and re-layouts, body(): kinds_base = jnp.where(real_atom, extended[3][safe_index], -1.0)  11.9 us
    all_to_all x1, starting transfers between devices, body(): lax.all_to_all(outbox.reshape(group_size, slot_cap, row_width), 'grp', sp...  11.1 us
    gather x2, local copies, waits for them, and re-layouts, body(): extended[:3][:, safe_index].reshape(3, frag_slots, frag_width)  10.9 us
  transfers between devices with their start and end apart: 11, of which 4 were waited for; matrix products, arithmetic and copies ran while one was open for 4% of the time, Pallas kernels for 0%

commit v1 on v0

v1 whole, which is shorter than its diff:
```python
import functools
import math

import jax
import jax.numpy as jnp
from jax import lax
from jax.experimental import pallas as pl
from jax.experimental.pallas import tpu as pltpu
from jax.sharding import PartitionSpec as P

HALO = 64
STEPS = 2
TIME_STEP = 0.05
NEAR_RATE = 0.5
FAR = 1e30
LANES = 128
GROUP = 4
F32 = jnp.float32
BF16 = jnp.bfloat16
HIGHEST = lax.Precision.HIGHEST


def dot_nn(a, b, precision=None):
    return lax.dot_general(
        a, b, (((1,), (0,)), ((), ())), precision=precision, preferred_element_type=F32
    )


def dot_nt(a, b):
    return lax.dot_general(a, b, (((1,), (1,)), ((), ())), preferred_element_type=F32)


def lane_pick(x, index):
    return jnp.take_along_axis(x, index, axis=1, mode="promise_in_bounds")


def iota(shape, dim):
    return lax.broadcasted_iota(jnp.int32, shape, dim)


def to_row(column):
    size = column.shape[0]
    same = iota((size, size), 0) == iota((size, size), 1)
    return jnp.sum(jnp.where(same, column, 0.0), axis=0, keepdims=True)


def to_column(row):
    size = row.shape[1]
    same = iota((size, size), 0) == iota((size, size), 1)
    return jnp.sum(jnp.where(same, row, 0.0), axis=1, keepdims=True)


def silu_of_double(half):
    return half + half * jnp.tanh(half)


def kernel(
    tiles,
    slots,
    heads,
    positions,
    velocities,
    masses,
    kinds,
    frag_atoms,
    assign,
    embed,
    neigh,
    w_query,
    w_key,
    w_value,
    w_energy,
    w_force,
    head_decay,
    positions_out,
    velocities_out,
    energies_out,
    ext,
    rim_out,
    rim_in,
    table,
    force_pad,
    rows,
    cols,
    counts,
    type_rows,
    pulls,
    atom_energy,
    send_sem,
    recv_sem,
):
    doms = lax.axis_size("dom")
    me = lax.axis_index("dom")
    upper, lower = lax.rem(me + 1, doms), lax.rem(me + doms - 1, doms)
    width = w_query.shape[0]
    head_width = width // heads
    ext_rows = ext.shape[1]
    types = embed.shape[0]

    barrier = pltpu.get_barrier_semaphore()
    for neighbour in (lower, upper):
        pl.semaphore_signal(
            barrier, inc=1, device_id={"dom": neighbour}, device_id_type=pl.DeviceIdType.MESH
        )

    lane = iota((slots, LANES), 1)

    for tile in range(tiles):
        span = pl.ds(tile * LANES, LANES)
        for c in range(3):
            ext[c, tile + 1 : tile + 2, :] = positions[c : c + 1, span]
            ext[4 + c, tile + 1 : tile + 2, :] = velocities[c : c + 1, span]
    ext[3, 1 : tiles + 1, :] = kinds[...].astype(F32)
    ext[7, 1 : tiles + 1, :] = masses[...]
    for c in range(8):
        ext[c, tiles + 2 : ext_rows, :] = jnp.full((ext_rows - tiles - 2, LANES), 1.0, F32)
    for side, row in ((0, tiles), (1, 1)):
        for c in range(8):
            rim_out[0, side, c : c + 1, :] = ext[c, row : row + 1, :]

    def exchange(phase):
        copies = []
        for side, target in ((0, upper), (1, lower)):
            copy = pltpu.make_async_remote_copy(
                src_ref=rim_out.at[phase, side],
                dst_ref=rim_in.at[phase, side],
                send_sem=send_sem.at[phase, side],
                recv_sem=recv_sem.at[phase, side],
                device_id={"dom": target},
                device_id_type=pl.DeviceIdType.MESH,
            )
            copy.start()
            copies.append(copy)
        return copies

    pl.semaphore_wait(barrier, 2)
    copies = exchange(0)

    table[...] = jnp.zeros(table.shape, F32)
    table[0:types, 0:width] = embed[...].astype(F32)
    table[0:types, width : 2 * width] = neigh[...].astype(F32)
    force_pad[...] = jnp.zeros(force_pad.shape, F32)
    force_pad[:, 0:heads] = w_force[...]
    readout = jnp.concatenate(
        [
            jnp.transpose(force_pad[...])[0:heads],
            w_energy[...],
            jnp.zeros((15 - heads, width), F32),
        ],
        axis=0,
    )
    readout_hi = readout.astype(BF16)
    readout = jnp.concatenate(
        [readout_hi, (readout - readout_hi.astype(F32)).astype(BF16)], axis=0
    )

    index = frag_atoms[...]
    live = jnp.where(index >= 0, 1.0, 0.0)
    active = to_column(jnp.where(assign[0:1, :] >= 0, 1.0, 0.0))
    count = jnp.sum(live, axis=1, keepdims=True) * active
    counts[...] = jnp.broadcast_to(count, (slots, LANES))
    start = jnp.maximum(index[:, 0:1], 0) + HALO
    tile_of = lax.shift_right_logical(start, 7)
    shift = jnp.bitwise_and(start, 127)
    both = jnp.concatenate([tile_of, tile_of + 1], axis=0)
    pick = jnp.where(iota((2 * slots, ext_rows), 1) == both, 1.0, 0.0)
    put = jnp.where(
        iota((ext_rows, 2 * slots), 0).astype(F32) == to_row(both.astype(F32)), 1.0, 0.0
    )
    atoms = frag_atoms.shape[1]
    half_lane = jnp.bitwise_and(lane, atoms - 1)
    ahead = half_lane + shift
    pick_lane = jnp.bitwise_and(ahead, 127)
    pick_first = ahead < LANES
    put_lane = jnp.bitwise_and(lane - shift, 127)
    put_first = lane >= shift

    sub8 = iota((8, LANES), 0)
    lane8 = iota((8, LANES), 1)
    lane64 = iota((atoms, LANES), 1)
    sub64 = iota((atoms, LANES), 0)
    left64 = lane64 < atoms
    other = jnp.bitwise_and(lane64, atoms - 1)
    latest = jnp.maximum(sub64, other).astype(F32)
    distinct = sub64 != other
    per_group = LANES // head_width
    groups = heads // per_group
    head_masks = [
        jnp.where(lax.shift_right_logical(lane64, 5) == h, 1.0, 0.0).astype(BF16)
        for h in range(per_group)
    ]
    decay_rows = [
        jnp.where(lane8 < atoms, -head_decay[2 * t], -head_decay[2 * t + 1])[0:1]
        for t in range(heads // 2)
    ]
    flat_masks = [
        jnp.where(sub8 == 2 * t + jnp.where(lane8 < atoms, 0, 1), 1.0, 0.0)
        for t in range(heads // 2)
    ]
    quarter = jnp.bitwise_and(sub8, 3)

    for copy in copies:
        copy.wait()
    for side, row in ((0, 0), (1, tiles + 1)):
        for c in range(8):
            ext[c, row : row + 1, :] = rim_in[0, side, c : c + 1, :]

    def gather(components):
        field = jnp.concatenate([ext[c] for c in components], axis=1)
        picked = dot_nn(pick, field, HIGHEST)
        result = []
        for c in range(len(components)):
            span = slice(c * LANES, (c + 1) * LANES)
            result.append(
                jnp.where(
                    pick_first,
                    lane_pick(picked[0:slots, span], pick_lane),
                    lane_pick(picked[slots:, span], pick_lane),
                )
            )
        return result

    def column(k):
        return lane_pick(cols[...], jnp.full((atoms, LANES), k, jnp.int32))

    def model(group, carry):
        many = range(GROUP)
        slot = [group * GROUP + k for k in many]
        base = pl.multiple_of(group * (GROUP * atoms), GROUP * atoms)
        xyz = [[rows[c, pl.ds(slot[k], 1), :] for c in range(3)] for k in many]
        far = []
        hidden = []
        for k in many:
            squared = None
            for c in range(3):
                spread = column(c * slots + slot[k]) - xyz[k][c]
                squared = spread * spread if squared is None else squared + spread * spread
            far.append(jnp.where(latest < counts[pl.ds(slot[k], 1), :], squared, FAR))
        for k in many:
            nearby = jnp.where(distinct, jnp.exp(-NEAR_RATE * far[k]), 0.0)
            near_hi = nearby.astype(BF16).astype(F32)
            near = jnp.where(left64, near_hi, nearby - near_hi).astype(BF16)
            span = pl.ds(base + k * atoms, atoms)
            theirs = type_rows[span, width : 2 * width]
            summed = dot_nn(near, jnp.concatenate([theirs, theirs], axis=0))
            summed = summed + type_rows[span, 0:width].astype(F32)
            hidden.append(silu_of_double(0.5 * summed).astype(BF16))
        block = jnp.concatenate(hidden, axis=0)
        query = dot_nn(block, w_query[...]).astype(BF16)
        key = dot_nn(block, w_key[...]).astype(BF16)
        value = dot_nn(block, w_value[...]).astype(BF16)
        weights = []
        for k in many:
            mine = slice(k * atoms, (k + 1) * atoms)
            parts = []
            for g in range(groups):
                span = slice(g * LANES, (g + 1) * LANES)
                keys = key[mine, span]
                spread_keys = jnp.concatenate([keys * mask for mask in head_masks], axis=0)
                parts.append(dot_nt(query[mine, span], spread_keys))
            tiles_out = []
            for t in range(heads // 2):
                part = parts[t // 2][:, (t % 2) * LANES : (t % 2 + 1) * LANES]
                half = part * (0.5 / math.sqrt(head_width))
                envelope = jnp.exp(far[k] * decay_rows[t])
                tiles_out.append((silu_of_double(half) * envelope).astype(BF16))
            weights.append(tiles_out)
        for k in many:
            mine = slice(k * atoms, (k + 1) * atoms)
            mixed = []
            for g in range(groups):
                span = slice(g * LANES, (g + 1) * LANES)
                values = value[mine, span]
                spread_values = jnp.concatenate([values * mask for mask in head_masks], axis=0)
                pair = jnp.concatenate(weights[k][2 * g : 2 * g + 2], axis=1)
                mixed.append(dot_nn(pair, spread_values))
            updated = hidden[k].astype(F32) + jnp.concatenate(mixed, axis=1)
            updated_hi = updated.astype(BF16)
            updated_lo = (updated - updated_hi.astype(F32)).astype(BF16)
            scalars = dot_nt(readout, jnp.concatenate([updated_hi, updated_lo], axis=0))
            scalars = scalars[0:16] + scalars[16:32]
            scalars = scalars + pltpu.roll(scalars, atoms, 1)
            atom_energy[pl.ds(slot[k], 1), :] = scalars[heads : heads + 1]
            spots = jnp.where(
                quarter == 0,
                1.0,
                jnp.where(
                    quarter == 1, xyz[k][0], jnp.where(quarter == 2, xyz[k][1], xyz[k][2])
                ),
            )
            left = []
            for t in range(heads // 2):
                flat = jnp.sum(scalars[0:heads] * flat_masks[t], axis=0, keepdims=True)
                term = flat * spots
                term_hi = term.astype(BF16).astype(F32)
                left.append(jnp.where(sub8 < 4, term_hi, term - term_hi))
            left = jnp.concatenate(left, axis=1)
            left = jnp.concatenate([left, jnp.zeros(left.shape, F32)], axis=0).astype(BF16)
            pulled = dot_nt(left, jnp.concatenate(weights[k], axis=1))
            pulls[slot[k], :, 0:atoms] = pulled[0:8]
        return carry

    for step in range(STEPS):
        fields = gather((0, 1, 2, 3) if step == 0 else (0, 1, 2))
        centred = [field - field[:, 0:1] for field in fields[:3]]
        for c in range(3):
            rows[c] = centred[c]
        if step == 0:
            sort = jnp.where(half_lane.astype(F32) < count, fields[3], -1.0)
        else:
            sort = centred[0]
        cols[...] = jnp.transpose(jnp.concatenate(centred + [sort], axis=0))[0:atoms]
        if step == 0:
            both_tables = table[...].astype(BF16)

            def look_up(group, carry):
                base = pl.multiple_of(group * (GROUP * atoms), GROUP * atoms)
                hot = jnp.concatenate(
                    [
                        jnp.where(
                            column(3 * slots + group * GROUP + k) == lane64.astype(F32), 1.0, 0.0
                        )
                        for k in range(GROUP)
                    ],
                    axis=0,
                ).astype(BF16)
                type_rows[pl.ds(base, GROUP * atoms), :] = dot_nn(hot, both_tables).astype(BF16)
                return carry

            lax.fori_loop(0, slots // GROUP, look_up, 0)
        lax.fori_loop(0, slots // GROUP, model, 0)

        energy = jnp.sum(jnp.where(lane < atoms, atom_energy[...], 0.0), axis=1, keepdims=True)
        energies_out[step : step + 1, :] = to_row(energy)
        sums = [pulls[:, q, :] + pulls[:, q + 4, :] for q in range(4)]
        firsts, seconds = [], []
        for c in range(3):
            force = jnp.where(lane < atoms, centred[c] * sums[0] - sums[c + 1], 0.0)
            turned = lane_pick(force, put_lane)
            firsts.append(jnp.where(put_first, turned, 0.0))
            seconds.append(jnp.where(put_first, 0.0, turned))
        placed = jnp.concatenate(
            [jnp.concatenate(firsts, axis=1), jnp.concatenate(seconds, axis=1)], axis=0
        )
        total = dot_nn(put, placed, HIGHEST)
        total = [total[:, c * LANES : (c + 1) * LANES] for c in range(3)]

        phase = step + 1
        for c in range(3):
            rim_out[phase, 0, c : c + 1, :] = total[c][tiles + 1 : tiles + 2]
            rim_out[phase, 0, c + 3 : c + 4, :] = total[c][tiles : tiles + 1]
            rim_out[phase, 1, c : c + 1, :] = total[c][0:1]
            rim_out[phase, 1, c + 3 : c + 4, :] = total[c][1:2]
        for side in range(2):
            rim_out[phase, side, 6:8, :] = jnp.zeros((2, LANES), F32)
        copies = exchange(phase)
        row_id = iota((ext_rows, LANES), 0)
        lane_id = iota((ext_rows, LANES), 1)
        from_lower = lane_id < HALO
        from_upper = lane_id >= LANES - HALO
        for copy in copies:
            copy.wait()
        for c in range(3):
            low = rim_in[phase, 0, c : c + 1, :]
            low_own = rim_in[phase, 0, c + 3 : c + 4, :]
            high = rim_in[phase, 1, c : c + 1, :]
            high_own = rim_in[phase, 1, c + 3 : c + 4, :]
            extra = jnp.where((row_id == 1) & from_lower, low, 0.0)
            extra = jnp.where((row_id == tiles) & from_upper, high, extra)
            extra = jnp.where((row_id == 0) & from_upper, low_own, extra)
            extra = jnp.where((row_id == tiles + 1) & from_lower, high_own, extra)
            moved = ext[4 + c] + TIME_STEP * (total[c] + extra) / ext[7]
            ext[4 + c] = moved
            ext[c] = ext[c] + TIME_STEP * moved

    for tile in range(tiles):
        span = pl.ds(tile * LANES, LANES)
        for c in range(3):
            positions_out[c : c + 1, span] = ext[c, tile + 1 : tile + 2, :]
            velocities_out[c : c + 1, span] = ext[4 + c, tile + 1 : tile + 2, :]


def body(
    positions,
    velocities,
    masses,
    atom_kinds,
    frag_atoms,
    assign,
    embed_table,
    neigh_table,
    w_query,
    w_key,
    w_value,
    w_energy,
    w_force,
    head_decay,
):
    tiles = positions.shape[1] // LANES
    slots, atoms = frag_atoms.shape
    heads = head_decay.shape[0]
    width = w_query.shape[0]
    ext_rows = -(-(tiles + 3) // 8) * 8
    vmem = pl.BlockSpec(memory_space=pltpu.VMEM)
    smem = pl.BlockSpec(memory_space=pltpu.SMEM)
    return pl.pallas_call(
        functools.partial(kernel, tiles, slots, heads),
        out_shape=(
            jax.ShapeDtypeStruct(positions.shape, F32),
            jax.ShapeDtypeStruct(velocities.shape, F32),
            jax.ShapeDtypeStruct((STEPS, slots), F32),
        ),
        in_specs=[vmem] * 13 + [smem],
        out_specs=(vmem, vmem, vmem),
        scratch_shapes=[
            pltpu.VMEM((8, ext_rows, LANES), F32),
            pltpu.VMEM((STEPS + 1, 2, 8, LANES), F32),
            pltpu.VMEM((STEPS + 1, 2, 8, LANES), F32),
            pltpu.VMEM((LANES, 2 * width), F32),
            pltpu.VMEM((width, LANES), F32),
            pltpu.VMEM((3, slots, LANES), F32),
            pltpu.VMEM((atoms, LANES), F32),
            pltpu.VMEM((slots, LANES), F32),
            pltpu.VMEM((slots * atoms, 2 * width), BF16),
            pltpu.VMEM((slots, 8, LANES), F32),
            pltpu.VMEM((slots, LANES), F32),
            pltpu.SemaphoreType.DMA((STEPS + 1, 2)),
            pltpu.SemaphoreType.DMA((STEPS + 1, 2)),
        ],
        compiler_params=pltpu.CompilerParams(
            collective_id=0, has_side_effects=True, vmem_limit_bytes=40 * 1024 * 1024
        ),
    )(
        positions,
        velocities,
        masses.reshape(tiles, LANES),
        atom_kinds.reshape(tiles, LANES),
        frag_atoms,
        assign,
        embed_table,
        neigh_table,
        w_query,
        w_key,
        w_value,
        w_energy.reshape(1, width),
        w_force,
        head_decay,
    )


def solution(mesh):
    both = ("dom", "grp")
    return jax.shard_map(
        body,
        mesh=mesh,
        in_specs=(
            P(None, both),
            P(None, both),
            P(both),
            P(both),
            P(both, None),
            P(None, both),
        )
        + (P(),) * 8,
        out_specs=(P(None, both), P(None, both), P(None, both)),
        check_vma=False,
    )
```

time: 255 us -> 74.7 us (0.29)
  the two profiles are of different devices: /device:TPU:1 before, /device:TPU:56 now
where the time goes in v1:
time: 74.7 us; the launch traced here: 74.1 us
  Pallas kernels  64.3 us (86%)
  local copies, waits for them, and re-layouts  9.06 us (12%)
    pallas_call x1, Pallas kernels, body(): pl.pallas_call(functools.partial(kernel, tiles, slots, heads), out_shape=...  64.3 us
    unnamed x30, local copies, waits for them, and re-layouts  9.06 us

profile of v1, /device:TPU:56, one launch (start us, length us, event | category | flops | bytes accessed | tf_op | source)
XLA Modules:
  0.0 74.1 jit_solution(1424282146561063360)
XLA Ops:
  0.6 0.0 copy-start
  0.6 0.0 copy-start.8
  0.7 0.0 copy-start.10
  0.7 0.0 copy-start.11
  0.7 0.0 copy-start.12
  0.7 0.9 %copy.17.w_force = f32[256,8]{1,0:T(8,128)S(1)} copy(f32[256,8]{0,1:T(8,128)} %param.26) | data formatting | bytes 16384 | tf_op args[12]
  1.6 0.0 copy-done
  1.6 0.0 copy-done.8
  1.6 0.0 copy-done.10
  1.6 0.0 copy-done.11
  1.6 0.0 copy-done.12
  1.6 0.0 copy-start.1
  1.6 0.9 %copy-done.1 = bf16[256,256]{1,0:T(8,128)(2,1)S(1)} copy-done((bf16[256,256]{1,0:T(8,128)(2,1)S(1)}, bf16[256,256]{1,0:T(8,128)(2,1)}, u32[]{:S(2)}) %copy-start.1) | copy-done | bytes 131096
  2.5 0.9 %copy-done.2 = bf16[256,256]{1,0:T(8,128)(2,1)S(1)} copy-done((bf16[256,256]{1,0:T(8,128)(2,1)S(1)}, bf16[256,256]{1,0:T(8,128)(2,1)}, u32[]{:S(2)}) %copy-start.2) | copy-done | bytes 131096
  3.4 0.8 %copy-done.3 = bf16[100,256]{1,0:T(8,128)(2,1)S(1)} copy-done((bf16[100,256]{1,0:T(8,128)(2,1)S(1)}, bf16[100,256]{1,0:T(8,128)(2,1)}, u32[]{:S(2)}) %copy-start.3) | copy-done | bytes 51224
  4.3 0.8 %copy-done.4 = bf16[100,256]{1,0:T(8,128)(2,1)S(1)} copy-done((bf16[100,256]{1,0:T(8,128)(2,1)S(1)}, bf16[100,256]{1,0:T(8,128)(2,1)}, u32[]{:S(2)}) %copy-start.4) | copy-done | bytes 51224
  5.1 0.8 %copy-done.5 = f32[3,2048]{1,0:T(4,128)S(1)} copy-done((f32[3,2048]{1,0:T(4,128)S(1)}, f32[3,2048]{1,0:T(4,128)}, u32[]{:S(2)}) %copy-start.5) | copy-done | bytes 24600
  5.8 0.8 %copy-done.6 = f32[3,2048]{1,0:T(4,128)S(1)} copy-done((f32[3,2048]{1,0:T(4,128)S(1)}, f32[3,2048]{1,0:T(4,128)}, u32[]{:S(2)}) %copy-start.6) | copy-done | bytes 24600
  6.6 0.7 copy-done.7
  7.3 0.7 copy-done.9
  8.0 64.3 %shard_map.157 = (f32[3,2048]{1,0:T(4,128)S(1)}, f32[3,2048]{1,0:T(4,128)S(1)}, f32[2,32]{1,0:T(2,128)S(1)}) custom-call(f32[3,2048]{1,0:T(4,128)S(1)} %copy-done.5, f32[3,2048]{1,0:T(4,128)S(1)} %copy-done.6, f32[16,128]{1,0:T(8,128)S(1)} %bitcast.3, s32[16,128]{1,0:T(8,128)S(1)} %bitcast.4, s32[32,64]{1,0:T(8,128)S(1)} %copy-done.7, ...), custom_call_target="tpu_custom_call" | custom-call | tf_op jit(solution)/shard_map/pallas_call | solution.py:406
  72.3 0.6 copy.21
  73.0 0.6 copy.22
  73.6 0.6 copy.23
  (7 shorter events, 0.0 us)
Async XLA Ops:
  0.6 1.0 %copy-start = (bf16[256,256]{1,0:T(8,128)(2,1)S(1)}, bf16[256,256]{1,0:T(8,128)(2,1)}, u32[]{:S(2)}) copy-start(bf16[256,256]{1,0:T(8,128)(2,1)} %w_query.1) | copy-start | bytes 393220
  0.6 1.0 %copy-start.8 = (f32[2048]{0:T(1024)S(1)}, f32[2048]{0:T(1024)}, u32[]{:S(2)}) copy-start(f32[2048]{0:T(1024)} %param.16) | copy-start | bytes 24580
  0.7 1.0 %copy-start.10 = (s32[2,32]{1,0:T(2,128)S(1)}, s32[2,32]{1,0:T(2,128)}, u32[]{:S(2)}) copy-start(s32[2,32]{1,0:T(2,128)} %assign.1) | copy-start | bytes 772
  0.7 1.0 %copy-start.11 = (f32[256]{0:T(256)S(1)}, f32[256]{0:T(256)}, u32[]{:S(2)}) copy-start(f32[256]{0:T(256)} %param.25) | copy-start | bytes 3076
  0.7 1.0 %copy-start.12 = (f32[8]{0:T(128)S(1)}, f32[8]{0:T(128)}, u32[]{:S(2)}) copy-start(f32[8]{0:T(128)} %head_decay.1) | copy-start | bytes 100
  1.6 0.9 %copy-start.1 = (bf16[256,256]{1,0:T(8,128)(2,1)S(1)}, bf16[256,256]{1,0:T(8,128)(2,1)}, u32[]{:S(2)}) copy-start(bf16[256,256]{1,0:T(8,128)(2,1)} %w_key.1) | copy-start | bytes 393220
  2.5 0.9 %copy-start.2 = (bf16[256,256]{1,0:T(8,128)(2,1)S(1)}, bf16[256,256]{1,0:T(8,128)(2,1)}, u32[]{:S(2)}) copy-start(bf16[256,256]{1,0:T(8,128)(2,1)} %w_value.1) | copy-start | bytes 393220
  3.4 0.8 %copy-start.3 = (bf16[100,256]{1,0:T(8,128)(2,1)S(1)}, bf16[100,256]{1,0:T(8,128)(2,1)}, u32[]{:S(2)}) copy-start(bf16[100,256]{1,0:T(8,128)(2,1)} %embed.1) | copy-start | bytes 153604
  4.3 0.8 %copy-start.4 = (bf16[100,256]{1,0:T(8,128)(2,1)S(1)}, bf16[100,256]{1,0:T(8,128)(2,1)}, u32[]{:S(2)}) copy-start(bf16[100,256]{1,0:T(8,128)(2,1)} %neigh.1) | copy-start | bytes 153604
  5.1 0.8 %copy-start.5 = (f32[3,2048]{1,0:T(4,128)S(1)}, f32[3,2048]{1,0:T(4,128)}, u32[]{:S(2)}) copy-start(f32[3,2048]{1,0:T(4,128)} %positions.1) | copy-start | bytes 73732
  5.8 0.8 %copy-start.6 = (f32[3,2048]{1,0:T(4,128)S(1)}, f32[3,2048]{1,0:T(4,128)}, u32[]{:S(2)}) copy-start(f32[3,2048]{1,0:T(4,128)} %velocities.1) | copy-start | bytes 73732
  6.6 0.7 copy-start.7
  7.3 0.7 copy-start.9

commit v2 on v1

v2 whole, which is shorter than its diff:
```python
import functools
import math

import jax
import jax.numpy as jnp
from jax import lax
from jax.experimental import pallas as pl
from jax.experimental.pallas import tpu as pltpu
from jax.sharding import PartitionSpec as P

HALO = 64
STEPS = 2
TIME_STEP = 0.05
NEAR_RATE = 0.5
FAR = 1e30
LANES = 128
UNROLL = 4
OPERANDS = 14
LOG2E = math.log2(math.e)
F32 = jnp.float32
BF16 = jnp.bfloat16


def dot_nn(a, b):
    return lax.dot_general(a, b, (((1,), (0,)), ((), ())), preferred_element_type=F32)


def dot_nt(a, b):
    return lax.dot_general(a, b, (((1,), (1,)), ((), ())), preferred_element_type=F32)


def lane_pick(x, index):
    return jnp.take_along_axis(x, index, axis=1, mode="promise_in_bounds")


def iota(shape, dim):
    return lax.broadcasted_iota(jnp.int32, shape, dim)


def to_row(column):
    size = column.shape[0]
    same = iota((size, size), 0) == iota((size, size), 1)
    return jnp.sum(jnp.where(same, column, 0.0), axis=0, keepdims=True)


def to_column(row):
    size = row.shape[1]
    same = iota((size, size), 0) == iota((size, size), 1)
    return jnp.sum(jnp.where(same, row, 0.0), axis=1, keepdims=True)


def silu_of_double(half):
    return half + half * jnp.tanh(half)


def kernel(tiles, slots, heads, *refs):
    operands, refs = refs[:OPERANDS], refs[OPERANDS:]
    (positions_out, velocities_out, energies_out), refs = refs[:3], refs[3:]
    local, refs = refs[:OPERANDS], refs[OPERANDS:]
    (
        ext,
        rim_out,
        rim_in,
        rows,
        cols,
        counts,
        spots,
        own_rows,
        neigh_rows,
        projections,
        head_readout,
        pulls,
        atom_energy,
        load_sem,
        send_sem,
        recv_sem,
    ) = refs
    loads = [
        pltpu.make_async_copy(source, target, load_sem.at[k])
        for k, (source, target) in enumerate(zip(operands, local))
    ]
    for load in loads:
        load.start()
    (
        positions,
        velocities,
        masses,
        kinds,
        frag_atoms,
        assign,
        embed,
        neigh,
        w_query,
        w_key,
        w_value,
        w_energy,
        w_force,
        head_decay,
    ) = local
    doms = lax.axis_size("dom")
    me = lax.axis_index("dom")
    upper, lower = lax.rem(me + 1, doms), lax.rem(me + doms - 1, doms)
    width = w_query.shape[0]
    head_width = width // heads
    ext_rows = ext.shape[1]
    types = embed.shape[0]

    barrier = pltpu.get_barrier_semaphore()
    for neighbour in (lower, upper):
        pl.semaphore_signal(
            barrier, inc=1, device_id={"dom": neighbour}, device_id_type=pl.DeviceIdType.MESH
        )

    lane = iota((slots, LANES), 1)

    for load in loads[:4]:
        load.wait()
    for tile in range(tiles):
        span = pl.ds(tile * LANES, LANES)
        for c in range(3):
            ext[c, tile + 1 : tile + 2, :] = positions[c : c + 1, span]
            ext[4 + c, tile + 1 : tile + 2, :] = velocities[c : c + 1, span]
    ext[3, 1 : tiles + 1, :] = kinds[...].astype(F32)
    ext[7, 1 : tiles + 1, :] = masses[...]
    for c in range(8):
        ext[c, tiles + 2 : ext_rows, :] = jnp.full((ext_rows - tiles - 2, LANES), 1.0, F32)
    for side, row in ((0, tiles), (1, 1)):
        for c in range(8):
            rim_out[0, side, c : c + 1, :] = ext[c, row : row + 1, :]

    def exchange(phase):
        copies = []
        for side, target in ((0, upper), (1, lower)):
            copy = pltpu.make_async_remote_copy(
                src_ref=rim_out.at[phase, side],
                dst_ref=rim_in.at[phase, side],
                send_sem=send_sem.at[phase, side],
                recv_sem=recv_sem.at[phase, side],
                device_id={"dom": target},
                device_id_type=pl.DeviceIdType.MESH,
            )
            copy.start()
            copies.append(copy)
        return copies

    pl.semaphore_wait(barrier, 2)
    copies = exchange(0)

    for load in loads[4:]:
        load.wait()
    readout = jnp.concatenate(
        [
            w_force[...],
            w_energy[...],
            jnp.zeros((15 - heads, width), F32),
        ],
        axis=0,
    )
    readout_hi = readout.astype(BF16).astype(F32)
    readout_lo = readout - readout_hi
    atoms = frag_atoms.shape[1]
    pairs = slots // 2
    projections[0:width] = jnp.transpose(w_key[...].astype(F32)).astype(BF16)
    projections[width : 2 * width] = jnp.transpose(w_value[...].astype(F32)).astype(BF16)
    projections[2 * width : 2 * width + 16] = readout_hi.astype(BF16)
    projections[2 * width + 16 : 2 * width + 32] = readout_lo.astype(BF16)
    feature_head = lax.shift_right_logical(iota((16, width), 1), 5)
    for h in range(heads):
        high, low = 16 * h, 16 * (heads + h)
        own = feature_head == h
        head_readout[high : high + 16] = jnp.where(own, readout_hi, 0.0).astype(BF16)
        head_readout[low : low + 16] = jnp.where(own, readout_lo, 0.0).astype(BF16)

    index = frag_atoms[...]
    live = jnp.where(index >= 0, 1.0, 0.0)
    active = to_column(jnp.where(assign[0:1, :] >= 0, 1.0, 0.0))
    count = jnp.sum(live, axis=1, keepdims=True) * active
    left_rows = iota((pairs, LANES), 1) < atoms
    counts[...] = jnp.where(left_rows, count[0:pairs], count[pairs:])
    start = jnp.maximum(index[:, 0:1], 0) + HALO
    tile_of = lax.shift_right_logical(start, 7)
    shift = jnp.bitwise_and(start, 127)
    both = jnp.concatenate([tile_of, tile_of + 1], axis=0)
    pick = jnp.where(iota((2 * slots, ext_rows), 1) == both, 1.0, 0.0)
    pick = jnp.concatenate([pick, pick, pick], axis=1).astype(BF16)
    put = jnp.where(
        iota((ext_rows, 2 * slots), 0).astype(F32) == to_row(both.astype(F32)), 1.0, 0.0
    )
    put = jnp.concatenate([put, put], axis=1).astype(BF16)
    half_lane = jnp.bitwise_and(lane, atoms - 1)
    ahead = half_lane + shift
    pick_lane = jnp.bitwise_and(ahead, 127)
    pick_first = ahead < LANES
    second = jnp.where(iota((slots, LANES), 0) < pairs, 0, atoms)
    put_lane = jnp.bitwise_and(lane - shift + second, 127)
    put_first = lane >= shift

    sub8 = iota((8, LANES), 0)
    lane8 = iota((8, LANES), 1)
    lane64 = iota((atoms, LANES), 1)
    sub64 = iota((atoms, LANES), 0)
    left8 = lane8 < atoms
    left16 = iota((16, LANES), 1) < atoms
    left64 = lane64 < atoms
    other = jnp.bitwise_and(lane64, atoms - 1)
    latest = jnp.maximum(sub64, other).astype(F32)
    distinct = sub64 != other
    member = jnp.where(left64, 0, pairs)
    keep_left = jnp.where(left64, 1.0, 0.0).astype(BF16)
    keep_right = jnp.where(left64, 0.0, 1.0).astype(BF16)
    per_group = LANES // head_width
    groups = heads // per_group
    half_scale = 0.5 / math.sqrt(head_width)
    decay_rows = [
        -LOG2E * jnp.where(left8[0:1], head_decay[:, 2 * t : 2 * t + 1], head_decay[:, 2 * t + 1 : 2 * t + 2])
        for t in range(heads // 2)
    ]
    flat_masks = [
        jnp.where(sub8 == 2 * t + jnp.where(left8, 0, 1), 1.0, 0.0) for t in range(heads // 2)
    ]
    empty = jnp.zeros((head_width, LANES), BF16)

    for copy in copies:
        copy.wait()
    for side, row in ((0, 0), (1, tiles + 1)):
        for c in range(8):
            ext[c, row : row + 1, :] = rim_in[0, side, c : c + 1, :]

    def gather(components):
        field = jnp.concatenate([ext[c] for c in components], axis=1)
        high = field.astype(BF16)
        rest = field - high.astype(F32)
        middle = rest.astype(BF16)
        low = (rest - middle.astype(F32)).astype(BF16)
        picked = dot_nn(pick, jnp.concatenate([high, middle, low], axis=0))
        result = []
        for c in range(len(components)):
            span = slice(c * LANES, (c + 1) * LANES)
            result.append(
                jnp.where(
                    pick_first,
                    lane_pick(picked[0:slots, span], pick_lane),
                    lane_pick(picked[slots:, span], pick_lane),
                )
            )
        return result

    def model(group, carry):
        first = group * (2 * UNROLL)
        mine = [first + k for k in range(2 * UNROLL)]
        many = range(2 * UNROLL)
        far, hidden = [], []
        for k in many:
            squared = None
            for c in range(3):
                column = lane_pick(cols[...], member + (c * slots + mine[k]))
                spread = column - rows[c, pl.ds(mine[k], 1), :]
                squared = spread * spread if squared is None else squared + spread * spread
            far.append(jnp.where(latest < counts[pl.ds(mine[k], 1), :], squared, FAR))
        summed = []
        for k in many:
            nearby = jnp.where(distinct, jnp.exp2((-NEAR_RATE * LOG2E) * far[k]), 0.0)
            near_hi = nearby.astype(BF16)
            near_lo = (nearby - near_hi.astype(F32)).astype(BF16)
            block = jnp.concatenate(
                [
                    jnp.concatenate([near * keep_left, near * keep_right], axis=0)
                    for near in (near_hi, near_lo)
                ],
                axis=1,
            )
            span = pl.ds(pl.multiple_of(mine[k] * LANES, LANES), LANES)
            theirs = neigh_rows[span, :]
            summed.append(dot_nn(block, jnp.concatenate([theirs, theirs], axis=0)))
        for k in many:
            span = pl.ds(pl.multiple_of(mine[k] * LANES, LANES), LANES)
            hidden.append(silu_of_double(summed[k] + own_rows[span, :]).astype(BF16))
        query, key, value, base = [], [], [], []
        for u in range(UNROLL):
            block = jnp.concatenate(hidden[2 * u : 2 * u + 2], axis=0)
            query.append(dot_nn(block, w_query[...]).astype(BF16))
            across = dot_nt(projections[...], block)
            key.append(across[0:width].astype(BF16))
            value.append(across[width : 2 * width].astype(BF16))
            base.append(across[2 * width : 2 * width + 16] + across[2 * width + 16 :])
        reads = [dot_nn(head_readout[...], value[u]) for u in range(UNROLL)]
        reads = [read[0 : 16 * heads] + read[16 * heads :] for read in reads]

        def scores(k):
            u, span = k // 2, slice((k % 2) * LANES, (k % 2 + 1) * LANES)
            straight = key[u][:, span]
            turned = pltpu.roll(straight, atoms, 1)
            result = []
            for m in range(2):
                at = (2 * (k % 2) + m) * atoms
                parts = []
                for g in range(groups):
                    blocks = []
                    for h in range(per_group):
                        feature = slice(
                            g * LANES + h * head_width, g * LANES + (h + 1) * head_width
                        )
                        source = straight if h % 2 == m else turned
                        keep = keep_left if h % 2 == 0 else keep_right
                        piece = source[feature] * keep[0:head_width]
                        blocks.append(
                            jnp.concatenate(
                                [piece if t == h // 2 else empty for t in range(per_group // 2)],
                                axis=1,
                            )
                        )
                    parts.append(
                        dot_nn(
                            query[u][at : at + atoms, g * LANES : (g + 1) * LANES],
                            jnp.concatenate(blocks, axis=0),
                        )
                    )
                result.append(parts)
            return result

        def weigh(k, parts):
            turned = pltpu.roll(far[k], atoms, 1)
            result = []
            for m in range(2):
                here = jnp.where(left64, far[k], turned) if m == 0 else jnp.where(left64, turned, far[k])
                tiles_out = []
                for t in range(heads // 2):
                    part = parts[m][t // 2][:, (t % 2) * LANES : (t % 2 + 1) * LANES]
                    envelope = jnp.exp2(here * decay_rows[t])
                    tiles_out.append((silu_of_double(part * half_scale) * envelope).astype(BF16))
                result.append(jnp.concatenate(tiles_out, axis=1))
            return jnp.concatenate(result, axis=0)

        weights = []
        ahead_scores = scores(0)
        for k in many:
            now = ahead_scores
            if k + 1 < 2 * UNROLL:
                ahead_scores = scores(k + 1)
            weights.append(weigh(k, now))
        mixed = []
        for k in many:
            u, span = k // 2, slice((k % 2) * LANES, (k % 2 + 1) * LANES)
            straight = reads[u][:, span]
            turned = pltpu.roll(straight, atoms, 1)
            left = []
            for m in range(2):
                a, b = (straight, turned) if m == 0 else (turned, straight)
                left.append(
                    jnp.concatenate(
                        [
                            jnp.where(
                                left16,
                                a[32 * t : 32 * t + 16],
                                b[32 * t + 16 : 32 * t + 32],
                            )
                            for t in range(heads // 2)
                        ],
                        axis=1,
                    )
                )
            left = jnp.concatenate(left, axis=0)
            left_hi = left.astype(BF16)
            left_lo = (left - left_hi.astype(F32)).astype(BF16)
            product = dot_nt(jnp.concatenate([left_hi, left_lo], axis=0), weights[k])
            mixed.append(product[0:32] + product[32:64])
        lefts = []
        for k in many:
            u, span = k // 2, slice((k % 2) * LANES, (k % 2 + 1) * LANES)
            scalars = jnp.where(left16, mixed[k][0:16], mixed[k][16:32]) + base[u][:, span]
            atom_energy[pl.ds(mine[k], 1), :] = scalars[heads : heads + 1]
            straight = scalars[0:heads]
            turned = pltpu.roll(straight, atoms, 1)
            left = []
            for m in range(2):
                a, b = (straight, turned) if m == 0 else (turned, straight)
                here = jnp.where(left8, a, b)
                place = spots[m * pairs + mine[k]]
                terms = []
                for t in range(heads // 2):
                    term = jnp.sum(here * flat_masks[t], axis=0, keepdims=True) * place
                    term_hi = term.astype(BF16).astype(F32)
                    terms.append(jnp.where(sub8 < 4, term_hi, term - term_hi))
                left.append(jnp.concatenate(terms, axis=1))
            lefts.append(jnp.concatenate(left, axis=0).astype(BF16))
        for k in many:
            pulled = dot_nt(lefts[k], weights[k])
            pulls[mine[k]] = jnp.where(left8, pulled[0:8], pulled[8:16])
        return carry

    for step in range(STEPS):
        fields = gather((0, 1, 2, 3) if step == 0 else (0, 1, 2))
        centred = [field - field[:, 0:1] for field in fields[:3]]
        for c in range(3):
            rows[c] = jnp.where(left_rows, centred[c][0:pairs], centred[c][pairs:])
            spots[:, c + 1, :] = centred[c]
            spots[:, c + 5, :] = centred[c]
        if step == 0:
            spots[:, 0, :] = jnp.ones((slots, LANES), F32)
            spots[:, 4, :] = jnp.ones((slots, LANES), F32)
            sort = jnp.where(half_lane.astype(F32) < count, fields[3], -1.0)
        else:
            sort = centred[0]
        cols[...] = jnp.transpose(jnp.concatenate(centred + [sort], axis=0))[0:atoms]
        if step == 0:
            both_tables = jnp.concatenate([embed[...] * 0.5, neigh[...] * 0.5], axis=1).astype(BF16)

            def look_up(group, carry):
                hot = []
                for k in range(2 * UNROLL):
                    for m in range(2):
                        at = 3 * slots + m * pairs + group * (2 * UNROLL) + k
                        kind = lane_pick(cols[...], jnp.full((atoms, LANES), at, jnp.int32))
                        hot.append(jnp.where(kind == lane64.astype(F32), 1.0, 0.0))
                hot = jnp.concatenate(hot, axis=0).astype(BF16)[:, 0:types]
                found = dot_nn(hot, both_tables)
                size = 2 * UNROLL * LANES
                span = pl.ds(pl.multiple_of(group * size, size), size)
                own_rows[span, :] = found[:, 0:width]
                neigh_rows[span, :] = found[:, width:].astype(BF16)
                return carry

            lax.fori_loop(0, pairs // (2 * UNROLL), look_up, 0)
        lax.fori_loop(0, pairs // (2 * UNROLL), model, 0)

        each = atom_energy[...]
        energy = jnp.concatenate(
            [
                jnp.sum(jnp.where(left_rows, each, 0.0), axis=1, keepdims=True),
                jnp.sum(jnp.where(left_rows, 0.0, each), axis=1, keepdims=True),
            ],
            axis=0,
        )
        energies_out[step : step + 1, :] = to_row(energy)
        sums = [pulls[:, q, :] + pulls[:, q + 4, :] for q in range(4)]
        firsts, seconds = [], []
        for c in range(3):
            force = rows[c] * sums[0] - sums[c + 1]
            force = jnp.concatenate(
                [jnp.where(left_rows, force, 0.0), jnp.where(left_rows, 0.0, force)], axis=0
            )
            turned = lane_pick(force, put_lane)
            firsts.append(jnp.where(put_first, turned, 0.0))
            seconds.append(jnp.where(put_first, 0.0, turned))
        placed = jnp.concatenate(
            [jnp.concatenate(firsts, axis=1), jnp.concatenate(seconds, axis=1)], axis=0
        )
        placed_hi = placed.astype(BF16)
        placed_lo = (placed - placed_hi.astype(F32)).astype(BF16)
        total = dot_nn(put, jnp.concatenate([placed_hi, placed_lo], axis=0))
        total = [total[:, c * LANES : (c + 1) * LANES] for c in range(3)]

        phase = step + 1
        for c in range(3):
            rim_out[phase, 0, c : c + 1, :] = total[c][tiles + 1 : tiles + 2]
            rim_out[phase, 0, c + 3 : c + 4, :] = total[c][tiles : tiles + 1]
            rim_out[phase, 1, c : c + 1, :] = total[c][0:1]
            rim_out[phase, 1, c + 3 : c + 4, :] = total[c][1:2]
        for side in range(2):
            rim_out[phase, side, 6:8, :] = jnp.zeros((2, LANES), F32)
        copies = exchange(phase)
        row_id = iota((ext_rows, LANES), 0)
        lane_id = iota((ext_rows, LANES), 1)
        from_lower = lane_id < HALO
        from_upper = lane_id >= LANES - HALO
        for copy in copies:
            copy.wait()
        for c in range(3):
            low = rim_in[phase, 0, c : c + 1, :]
            low_own = rim_in[phase, 0, c + 3 : c + 4, :]
            high = rim_in[phase, 1, c : c + 1, :]
            high_own = rim_in[phase, 1, c + 3 : c + 4, :]
            extra = jnp.where((row_id == 1) & from_lower, low, 0.0)
            extra = jnp.where((row_id == tiles) & from_upper, high, extra)
            extra = jnp.where((row_id == 0) & from_upper, low_own, extra)
            extra = jnp.where((row_id == tiles + 1) & from_lower, high_own, extra)
            moved = ext[4 + c] + TIME_STEP * (total[c] + extra) / ext[7]
            ext[4 + c] = moved
            ext[c] = ext[c] + TIME_STEP * moved

    for tile in range(tiles):
        span = pl.ds(tile * LANES, LANES)
        for c in range(3):
            positions_out[c : c + 1, span] = ext[c, tile + 1 : tile + 2, :]
            velocities_out[c : c + 1, span] = ext[4 + c, tile + 1 : tile + 2, :]


def hand_over(*refs):
    for k in range(3):
        refs[k + 3][...] = refs[k][...]


def body(
    positions,
    velocities,
    masses,
    atom_kinds,
    frag_atoms,
    assign,
    embed_table,
    neigh_table,
    w_query,
    w_key,
    w_value,
    w_energy,
    w_force,
    head_decay,
):
    tiles = positions.shape[1] // LANES
    slots, atoms = frag_atoms.shape
    heads = head_decay.shape[0]
    width = w_query.shape[0]
    ext_rows = -(-(tiles + 3) // 8) * 8
    vmem = pl.BlockSpec(memory_space=pltpu.VMEM)
    operands = (
        positions,
        velocities,
        masses.reshape(tiles, LANES),
        atom_kinds.reshape(tiles, LANES),
        frag_atoms,
        assign,
        embed_table,
        neigh_table,
        w_query,
        w_key,
        w_value,
        w_energy.reshape(1, width),
        w_force.T,
        head_decay.reshape(1, heads),
    )
    results = pl.pallas_call(
        functools.partial(kernel, tiles, slots, heads),
        out_shape=(
            jax.ShapeDtypeStruct(positions.shape, F32),
            jax.ShapeDtypeStruct(velocities.shape, F32),
            jax.ShapeDtypeStruct((STEPS, slots), F32),
        ),
        in_specs=[pl.BlockSpec(memory_space=pltpu.HBM)] * OPERANDS,
        out_specs=(vmem, vmem, vmem),
        scratch_shapes=[pltpu.VMEM(operand.shape, operand.dtype) for operand in operands]
        + [
            pltpu.VMEM((8, ext_rows, LANES), F32),
            pltpu.VMEM((STEPS + 1, 2, 8, LANES), F32),
            pltpu.VMEM((STEPS + 1, 2, 8, LANES), F32),
            pltpu.VMEM((3, slots // 2, LANES), F32),
            pltpu.VMEM((atoms, LANES), F32),
            pltpu.VMEM((slots // 2, LANES), F32),
            pltpu.VMEM((slots, 8, LANES), F32),
            pltpu.VMEM((slots * atoms, width), F32),
            pltpu.VMEM((slots * atoms, width), BF16),
            pltpu.VMEM((2 * width + 32, width), BF16),
            pltpu.VMEM((32 * heads, width), BF16),
            pltpu.VMEM((slots // 2, 8, LANES), F32),
            pltpu.VMEM((slots // 2, LANES), F32),
            pltpu.SemaphoreType.DMA((OPERANDS,)),
            pltpu.SemaphoreType.DMA((STEPS + 1, 2)),
            pltpu.SemaphoreType.DMA((STEPS + 1, 2)),
        ],
        compiler_params=pltpu.CompilerParams(
            collective_id=0, has_side_effects=True, vmem_limit_bytes=56 * 1024 * 1024
        ),
    )(*operands)
    return pl.pallas_call(
        hand_over,
        out_shape=tuple(jax.ShapeDtypeStruct(result.shape, F32) for result in results),
        in_specs=[vmem] * 3,
        out_specs=(vmem,) * 3,
        compiler_params=pltpu.CompilerParams(vmem_limit_bytes=56 * 1024 * 1024),
    )(*results)


def solution(mesh):
    both = ("dom", "grp")
    return jax.shard_map(
        body,
        mesh=mesh,
        in_specs=(
            P(None, both),
            P(None, both),
            P(both),
            P(both),
            P(both, None),
            P(None, both),
        )
        + (P(),) * 8,
        out_specs=(P(None, both), P(None, both), P(None, both)),
        check_vma=False,
    )
```

time: 74.7 us -> 38.5 us (0.52)
  Pallas kernels: 64.3 us -> 37.6 us
  local copies, waits for them, and re-layouts: 9.06 us -> 0 us
    pallas_call x1, Pallas kernels: 64.3 us -> 36.2 us  [body(): pl.pallas_call(functools.partial(kernel, tiles, slots, heads), out_shape=...]
    unnamed x30 -> x0, local copies, waits for them, and re-layouts: 9.06 us -> none
    pallas_call x0 -> x1, Pallas kernels: none -> 1.41 us  [body(): pl.pallas_call(hand_over, out_shape=tuple((jax.ShapeDtypeStruct(result.sh...]
where the time goes in v2:
time: 38.5 us; the launch traced here: 38.3 us
  Pallas kernels  37.6 us (98%)
  between operations  0.64 us (2%)
    pallas_call x1, Pallas kernels, body(): pl.pallas_call(functools.partial(kernel, tiles, slots, heads), out_shape=...  36.2 us
    pallas_call x1, Pallas kernels, body(): pl.pallas_call(hand_over, out_shape=tuple((jax.ShapeDtypeStruct(result.sh...  1.41 us

profile of v2, /device:TPU:56, one launch (start us, length us, event | category | flops | bytes accessed | tf_op | source)
XLA Modules:
  0.0 38.3 jit_solution(2565850547909875617)
XLA Ops:
  0.6 36.2 %shard_map.157 = (f32[3,2048]{1,0:T(4,128)}, f32[3,2048]{1,0:T(4,128)}, f32[2,32]{1,0:T(2,128)}) custom-call(f32[3,2048]{1,0:T(4,128)} %refs_0_.1, f32[3,2048]{1,0:T(4,128)} %refs_1_.1, f32[16,128]{1,0:T(8,128)} %bitcast.5, s32[16,128]{1,0:T(8,128)} %bitcast.6, s32[32,64]{1,0:T(8,128)} %refs_4_.1, s32[2,32]{1,0:T(2,128)} %refs_5_.1, ...), custom_call_target="tpu_custom_call" | custom-call | tf_op jit(solution)/shard_map/pallas_call | solution.py:531
  36.9 1.4 %shard_map.158 = (f32[3,2048]{1,0:T(4,128)}, f32[3,2048]{1,0:T(4,128)}, f32[2,32]{1,0:T(2,128)}) custom-call(f32[3,2048]{1,0:T(4,128)} %get-tuple-element.6.refs_0_, f32[3,2048]{1,0:T(4,128)} %get-tuple-element.7.refs_1_, f32[2,32]{1,0:T(2,128)} %get-tuple-element.8.refs_2_), custom_call_target="tpu_custom_call" | custom-call | tf_op jit(solution)/shard_map/pallas_call | solution.py:563

commit v3 on v2

--- a/solution.py
+++ b/solution.py
@@ -14,9 +14,8 @@
 NEAR_RATE = 0.5
 FAR = 1e30
 LANES = 128
-UNROLL = 4
+TERMS = 24
 OPERANDS = 14
-LOG2E = math.log2(math.e)
 F32 = jnp.float32
 BF16 = jnp.bfloat16
 
@@ -71,6 +70,8 @@
         head_readout,
         pulls,
         atom_energy,
+        firsts,
+        seconds,
         load_sem,
         send_sem,
         recv_sem,
@@ -115,18 +116,12 @@
 
     for load in loads[:4]:
         load.wait()
-    for tile in range(tiles):
+    for side, tile in ((0, tiles - 1), (1, 0)):
         span = pl.ds(tile * LANES, LANES)
-        for c in range(3):
-            ext[c, tile + 1 : tile + 2, :] = positions[c : c + 1, span]
-            ext[4 + c, tile + 1 : tile + 2, :] = velocities[c : c + 1, span]
-    ext[3, 1 : tiles + 1, :] = kinds[...].astype(F32)
-    ext[7, 1 : tiles + 1, :] = masses[...]
-    for c in range(8):
-        ext[c, tiles + 2 : ext_rows, :] = jnp.full((ext_rows - tiles - 2, LANES), 1.0, F32)
-    for side, row in ((0, tiles), (1, 1)):
-        for c in range(8):
-            rim_out[0, side, c : c + 1, :] = ext[c, row : row + 1, :]
+        rim_out[0, side, 0:3, :] = positions[:, span]
+        rim_out[0, side, 3:4, :] = kinds[tile : tile + 1, :].astype(F32)
+        rim_out[0, side, 4:7, :] = velocities[:, span]
+        rim_out[0, side, 7:8, :] = masses[tile : tile + 1, :]
 
     def exchange(phase):
         copies = []
@@ -145,6 +140,19 @@
 
     pl.semaphore_wait(barrier, 2)
     copies = exchange(0)
+
+    for tile in range(tiles):
+        span = pl.ds(tile * LANES, LANES)
+        for c in range(3):
+            ext[c, tile + 1 : tile + 2, :] = positions[c : c + 1, span]
+            ext[4 + c, tile + 1 : tile + 2, :] = velocities[c : c + 1, span]
+    ext[3, 1 : tiles + 1, :] = kinds[...].astype(F32)
+    ext[7, 1 : tiles + 1, :] = masses[...]
+    for c in range(8):
+        ext[c, tiles + 2 : ext_rows, :] = jnp.full((ext_rows - tiles - 2, LANES), 1.0, F32)
+    for phase in range(1, STEPS + 1):
+        for side in range(2):
+            rim_out[phase, side, 6:8, :] = jnp.zeros((2, LANES), F32)
 
     for load in loads[4:]:
         load.wait()
@@ -205,14 +213,13 @@
     other = jnp.bitwise_and(lane64, atoms - 1)
     latest = jnp.maximum(sub64, other).astype(F32)
     distinct = sub64 != other
-    member = jnp.where(left64, 0, pairs)
     keep_left = jnp.where(left64, 1.0, 0.0).astype(BF16)
     keep_right = jnp.where(left64, 0.0, 1.0).astype(BF16)
     per_group = LANES // head_width
     groups = heads // per_group
     half_scale = 0.5 / math.sqrt(head_width)
     decay_rows = [
-        -LOG2E * jnp.where(left8[0:1], head_decay[:, 2 * t : 2 * t + 1], head_decay[:, 2 * t + 1 : 2 * t + 2])
+        -jnp.where(left8[0:1], head_decay[:, 2 * t : 2 * t + 1], head_decay[:, 2 * t + 1 : 2 * t + 2])
         for t in range(heads // 2)
     ]
     flat_masks = [
@@ -225,6 +232,8 @@
     for side, row in ((0, 0), (1, tiles + 1)):
         for c in range(8):
             ext[c, row : row + 1, :] = rim_in[0, side, c : c + 1, :]
+    ext[7] = TIME_STEP / ext[7]
+    shared = (iota((2, LANES), 0) == 0) == (iota((2, LANES), 1) >= HALO)
 
     def gather(components):
         field = jnp.concatenate([ext[c] for c in components], axis=1)
@@ -245,21 +254,52 @@
             )
         return result
 
-    def model(group, carry):
-        first = group * (2 * UNROLL)
-        mine = [first + k for k in range(2 * UNROLL)]
-        many = range(2 * UNROLL)
+    quads = pairs // 2
+    many = range(pairs)
+    nothing = jnp.zeros((2 * TERMS, LANES), BF16)
+
+    def set_distances(centred):
+        def parts(x):
+            high = x.astype(BF16).astype(F32)
+            middle = (x - high).astype(BF16).astype(F32)
+            return high, middle, x - high - middle
+
+        ones = jnp.ones((slots, LANES), F32)
+        terms = []
+        norm = None
+        for x in centred:
+            norm = x * x if norm is None else norm + x * x
+            h, m, l = parts(x)
+            terms += [(h, h), (h, m), (m, h), (h, l), (l, h), (m, m)]
+        terms = [(-2.0 * a, b) for a, b in terms]
+        for n in parts(norm):
+            terms += [(n, ones), (ones, n)]
+        for k, (a, b) in enumerate(terms):
+            firsts[:, k, :] = a[0:pairs]
+            firsts[:, TERMS + k, :] = a[pairs:]
+            seconds[:, k, :] = jnp.where(left_rows, b[0:pairs], 0.0)
+            seconds[:, TERMS + k, :] = jnp.where(left_rows, 0.0, b[pairs:])
+
+    def model():
         far, hidden = [], []
-        for k in many:
-            squared = None
-            for c in range(3):
-                column = lane_pick(cols[...], member + (c * slots + mine[k]))
-                spread = column - rows[c, pl.ds(mine[k], 1), :]
-                squared = spread * spread if squared is None else squared + spread * spread
-            far.append(jnp.where(latest < counts[pl.ds(mine[k], 1), :], squared, FAR))
+        for u in range(quads):
+            both = firsts[2 * u : 2 * u + 2].reshape(4 * TERMS, LANES)
+            left = jnp.transpose(both)[0:atoms].astype(BF16)
+            right = [seconds[2 * u + v].astype(BF16) for v in range(2)]
+            right = jnp.concatenate(
+                [
+                    jnp.concatenate([right[0], nothing], axis=0),
+                    jnp.concatenate([nothing, right[1]], axis=0),
+                ],
+                axis=1,
+            )
+            squared = dot_nn(left, right)
+            for v in range(2):
+                inside = latest < counts[2 * u + v : 2 * u + v + 1, :]
+                far.append(jnp.where(inside, squared[:, v * LANES : (v + 1) * LANES], FAR))
         summed = []
         for k in many:
-            nearby = jnp.where(distinct, jnp.exp2((-NEAR_RATE * LOG2E) * far[k]), 0.0)
+            nearby = jnp.where(distinct, jnp.exp(-NEAR_RATE * far[k]), 0.0)
             near_hi = nearby.astype(BF16)
             near_lo = (nearby - near_hi.astype(F32)).astype(BF16)
             block = jnp.concatenate(
@@ -269,21 +309,21 @@
                 ],
                 axis=1,
             )
-            span = pl.ds(pl.multiple_of(mine[k] * LANES, LANES), LANES)
+            span = slice(k * LANES, (k + 1) * LANES)
             theirs = neigh_rows[span, :]
             summed.append(dot_nn(block, jnp.concatenate([theirs, theirs], axis=0)))
         for k in many:
-            span = pl.ds(pl.multiple_of(mine[k] * LANES, LANES), LANES)
+            span = slice(k * LANES, (k + 1) * LANES)
             hidden.append(silu_of_double(summed[k] + own_rows[span, :]).astype(BF16))
         query, key, value, base = [], [], [], []
-        for u in range(UNROLL):
+        for u in range(quads):
             block = jnp.concatenate(hidden[2 * u : 2 * u + 2], axis=0)
             query.append(dot_nn(block, w_query[...]).astype(BF16))
             across = dot_nt(projections[...], block)
             key.append(across[0:width].astype(BF16))
             value.append(across[width : 2 * width].astype(BF16))
             base.append(across[2 * width : 2 * width + 16] + across[2 * width + 16 :])
-        reads = [dot_nn(head_readout[...], value[u]) for u in range(UNROLL)]
+        reads = [dot_nn(head_readout[...], value[u]) for u in range(quads)]
         reads = [read[0 : 16 * heads] + read[16 * heads :] for read in reads]
 
         def scores(k):
@@ -326,7 +366,7 @@
                 tiles_out = []
                 for t in range(heads // 2):
                     part = parts[m][t // 2][:, (t % 2) * LANES : (t % 2 + 1) * LANES]
-                    envelope = jnp.exp2(here * decay_rows[t])
+                    envelope = jnp.exp(here * decay_rows[t])
                     tiles_out.append((silu_of_double(part * half_scale) * envelope).astype(BF16))
                 result.append(jnp.concatenate(tiles_out, axis=1))
             return jnp.concatenate(result, axis=0)
@@ -335,7 +375,7 @@
         ahead_scores = scores(0)
         for k in many:
             now = ahead_scores
-            if k + 1 < 2 * UNROLL:
+            if k + 1 < pairs:
                 ahead_scores = scores(k + 1)
             weights.append(weigh(k, now))
         mixed = []
@@ -368,14 +408,14 @@
         for k in many:
             u, span = k // 2, slice((k % 2) * LANES, (k % 2 + 1) * LANES)
             scalars = jnp.where(left16, mixed[k][0:16], mixed[k][16:32]) + base[u][:, span]
-            atom_energy[pl.ds(mine[k], 1), :] = scalars[heads : heads + 1]
+            atom_energy[k : k + 1, :] = scalars[heads : heads + 1]
             straight = scalars[0:heads]
             turned = pltpu.roll(straight, atoms, 1)
             left = []
             for m in range(2):
                 a, b = (straight, turned) if m == 0 else (turned, straight)
                 here = jnp.where(left8, a, b)
-                place = spots[m * pairs + mine[k]]
+                place = spots[m * pairs + k]
                 terms = []
                 for t in range(heads // 2):
                     term = jnp.sum(here * flat_masks[t], axis=0, keepdims=True) * place
@@ -385,44 +425,9 @@
             lefts.append(jnp.concatenate(left, axis=0).astype(BF16))
         for k in many:
             pulled = dot_nt(lefts[k], weights[k])
-            pulls[mine[k]] = jnp.where(left8, pulled[0:8], pulled[8:16])
-        return carry
-
-    for step in range(STEPS):
-        fields = gather((0, 1, 2, 3) if step == 0 else (0, 1, 2))
-        centred = [field - field[:, 0:1] for field in fields[:3]]
-        for c in range(3):
-            rows[c] = jnp.where(left_rows, centred[c][0:pairs], centred[c][pairs:])
-            spots[:, c + 1, :] = centred[c]
-            spots[:, c + 5, :] = centred[c]
-        if step == 0:
-            spots[:, 0, :] = jnp.ones((slots, LANES), F32)
-            spots[:, 4, :] = jnp.ones((slots, LANES), F32)
-            sort = jnp.where(half_lane.astype(F32) < count, fields[3], -1.0)
-        else:
-            sort = centred[0]
-        cols[...] = jnp.transpose(jnp.concatenate(centred + [sort], axis=0))[0:atoms]
-        if step == 0:
-            both_tables = jnp.concatenate([embed[...] * 0.5, neigh[...] * 0.5], axis=1).astype(BF16)
-
-            def look_up(group, carry):
-                hot = []
-                for k in range(2 * UNROLL):
-                    for m in range(2):
-                        at = 3 * slots + m * pairs + group * (2 * UNROLL) + k
-                        kind = lane_pick(cols[...], jnp.full((atoms, LANES), at, jnp.int32))
-                        hot.append(jnp.where(kind == lane64.astype(F32), 1.0, 0.0))
-                hot = jnp.concatenate(hot, axis=0).astype(BF16)[:, 0:types]
-                found = dot_nn(hot, both_tables)
-                size = 2 * UNROLL * LANES
-                span = pl.ds(pl.multiple_of(group * size, size), size)
-                own_rows[span, :] = found[:, 0:width]
-                neigh_rows[span, :] = found[:, width:].astype(BF16)
-                return carry
-
-            lax.fori_loop(0, pairs // (2 * UNROLL), look_up, 0)
-        lax.fori_loop(0, pairs // (2 * UNROLL), model, 0)
-
+            pulls[k] = jnp.where(left8, pulled[0:8], pulled[8:16])
+
+    def finish_energy(step):
         each = atom_energy[...]
         energy = jnp.concatenate(
             [
@@ -432,18 +437,55 @@
             axis=0,
         )
         energies_out[step : step + 1, :] = to_row(energy)
+
+    def hand_out(which):
+        for tile in which:
+            span = pl.ds(tile * LANES, LANES)
+            for c in range(3):
+                positions_out[c : c + 1, span] = ext[c, tile + 1 : tile + 2, :]
+                velocities_out[c : c + 1, span] = ext[4 + c, tile + 1 : tile + 2, :]
+
+    for step in range(STEPS):
+        fields = gather((0, 1, 2, 3) if step == 0 else (0, 1, 2))
+        centred = [field - field[:, 0:1] for field in fields[:3]]
+        for c in range(3):
+            rows[c] = jnp.where(left_rows, centred[c][0:pairs], centred[c][pairs:])
+            spots[:, c + 1, :] = centred[c]
+            spots[:, c + 5, :] = centred[c]
+        set_distances(centred)
+        if step == 0:
+            spots[:, 0, :] = jnp.ones((slots, LANES), F32)
+            spots[:, 4, :] = jnp.ones((slots, LANES), F32)
+            sort = jnp.where(half_lane.astype(F32) < count, fields[3], -1.0)
+            cols[...] = jnp.transpose(jnp.concatenate([sort] * (LANES // slots), axis=0))[0:atoms]
+            both_tables = jnp.concatenate([embed[...] * 0.5, neigh[...] * 0.5], axis=1).astype(BF16)
+
+            for u in range(quads):
+                hot = []
+                for k in (2 * u, 2 * u + 1):
+                    for m in range(2):
+                        at = jnp.full((atoms, LANES), m * pairs + k, jnp.int32)
+                        kind = lane_pick(cols[...], at)
+                        hot.append(jnp.where(kind == lane64.astype(F32), 1.0, 0.0))
+                hot = jnp.concatenate(hot, axis=0).astype(BF16)[:, 0:types]
+                found = dot_nn(hot, both_tables)
+                span = slice(2 * u * LANES, (2 * u + 2) * LANES)
+                own_rows[span, :] = found[:, 0:width]
+                neigh_rows[span, :] = found[:, width:].astype(BF16)
+        model()
+
         sums = [pulls[:, q, :] + pulls[:, q + 4, :] for q in range(4)]
-        firsts, seconds = [], []
+        placed_here, placed_next = [], []
         for c in range(3):
             force = rows[c] * sums[0] - sums[c + 1]
             force = jnp.concatenate(
                 [jnp.where(left_rows, force, 0.0), jnp.where(left_rows, 0.0, force)], axis=0
             )
             turned = lane_pick(force, put_lane)
-            firsts.append(jnp.where(put_first, turned, 0.0))
-            seconds.append(jnp.where(put_first, 0.0, turned))
+            placed_here.append(jnp.where(put_first, turned, 0.0))
+            placed_next.append(jnp.where(put_first, 0.0, turned))
         placed = jnp.concatenate(
-            [jnp.concatenate(firsts, axis=1), jnp.concatenate(seconds, axis=1)], axis=0
+            [jnp.concatenate(placed_here, axis=1), jnp.concatenate(placed_next, axis=1)], axis=0
         )
         placed_hi = placed.astype(BF16)
         placed_lo = (placed - placed_hi.astype(F32)).astype(BF16)
@@ -452,37 +494,26 @@
 
         phase = step + 1
         for c in range(3):
-            rim_out[phase, 0, c : c + 1, :] = total[c][tiles + 1 : tiles + 2]
-            rim_out[phase, 0, c + 3 : c + 4, :] = total[c][tiles : tiles + 1]
-            rim_out[phase, 1, c : c + 1, :] = total[c][0:1]
-            rim_out[phase, 1, c + 3 : c + 4, :] = total[c][1:2]
-        for side in range(2):
-            rim_out[phase, side, 6:8, :] = jnp.zeros((2, LANES), F32)
+            rim_out[phase, 0, 2 * c : 2 * c + 2, :] = total[c][tiles : tiles + 2]
+            rim_out[phase, 1, 2 * c : 2 * c + 2, :] = total[c][0:2]
         copies = exchange(phase)
-        row_id = iota((ext_rows, LANES), 0)
-        lane_id = iota((ext_rows, LANES), 1)
-        from_lower = lane_id < HALO
-        from_upper = lane_id >= LANES - HALO
+        for c in range(3):
+            moved = ext[4 + c] + total[c] * ext[7]
+            ext[4 + c] = moved
+            ext[c] = ext[c] + TIME_STEP * moved
+        finish_energy(step)
+        if step == STEPS - 1:
+            hand_out(range(1, tiles - 1))
         for copy in copies:
             copy.wait()
-        for c in range(3):
-            low = rim_in[phase, 0, c : c + 1, :]
-            low_own = rim_in[phase, 0, c + 3 : c + 4, :]
-            high = rim_in[phase, 1, c : c + 1, :]
-            high_own = rim_in[phase, 1, c + 3 : c + 4, :]
-            extra = jnp.where((row_id == 1) & from_lower, low, 0.0)
-            extra = jnp.where((row_id == tiles) & from_upper, high, extra)
-            extra = jnp.where((row_id == 0) & from_upper, low_own, extra)
-            extra = jnp.where((row_id == tiles + 1) & from_lower, high_own, extra)
-            moved = ext[4 + c] + TIME_STEP * (total[c] + extra) / ext[7]
-            ext[4 + c] = moved
-            ext[c] = ext[c] + TIME_STEP * moved
-
-    for tile in range(tiles):
-        span = pl.ds(tile * LANES, LANES)
-        for c in range(3):
-            positions_out[c : c + 1, span] = ext[c, tile + 1 : tile + 2, :]
-            velocities_out[c : c + 1, span] = ext[4 + c, tile + 1 : tile + 2, :]
+        for side, row in ((0, 0), (1, tiles)):
+            border = slice(row, row + 2)
+            for c in range(3):
+                extra = jnp.where(shared, rim_in[phase, side, 2 * c : 2 * c + 2, :], 0.0)
+                kick = extra * ext[7, border, :]
+                ext[4 + c, border, :] = ext[4 + c, border, :] + kick
+                ext[c, border, :] = ext[c, border, :] + TIME_STEP * kick
+    hand_out((0, tiles - 1))
 
 
 def hand_over(*refs):
@@ -552,6 +583,8 @@
             pltpu.VMEM((32 * heads, width), BF16),
             pltpu.VMEM((slots // 2, 8, LANES), F32),
             pltpu.VMEM((slots // 2, LANES), F32),
+            pltpu.VMEM((slots // 2, 2 * TERMS, LANES), F32),
+            pltpu.VMEM((slots // 2, 2 * TERMS, LANES), F32),
             pltpu.SemaphoreType.DMA((OPERANDS,)),
             pltpu.SemaphoreType.DMA((STEPS + 1, 2)),
             pltpu.SemaphoreType.DMA((STEPS + 1, 2)),

time: 38.5 us -> 37.3 us (0.969)
  Pallas kernels: 37.6 us -> 36.4 us
    pallas_call x1, Pallas kernels: 36.2 us -> 35 us  [body(): pl.pallas_call(functools.partial(kernel, tiles, slots, heads), out_shape=...]
where the time goes in v3:
time: 37.3 us; the launch traced here: 37 us
  Pallas kernels  36.4 us (98%)
  between operations  0.64 us (2%)
    pallas_call x1, Pallas kernels, body(): pl.pallas_call(functools.partial(kernel, tiles, slots, heads), out_shape=...  35 us
    pallas_call x1, Pallas kernels, body(): pl.pallas_call(hand_over, out_shape=tuple((jax.ShapeDtypeStruct(result.sh...  1.41 us

profile of v3, /device:TPU:56, one launch (start us, length us, event | category | flops | bytes accessed | tf_op | source)
XLA Modules:
  0.0 37.0 jit_solution(179703016803183050)
XLA Ops:
  0.6 35.0 %shard_map.157 = (f32[3,2048]{1,0:T(4,128)}, f32[3,2048]{1,0:T(4,128)}, f32[2,32]{1,0:T(2,128)}) custom-call(f32[3,2048]{1,0:T(4,128)} %refs_0_.1, f32[3,2048]{1,0:T(4,128)} %refs_1_.1, f32[16,128]{1,0:T(8,128)} %bitcast.5, s32[16,128]{1,0:T(8,128)} %bitcast.6, s32[32,64]{1,0:T(8,128)} %refs_4_.1, s32[2,32]{1,0:T(2,128)} %refs_5_.1, ...), custom_call_target="tpu_custom_call" | custom-call | tf_op jit(solution)/shard_map/pallas_call | solution.py:562
  35.6 1.4 %shard_map.158 = (f32[3,2048]{1,0:T(4,128)}, f32[3,2048]{1,0:T(4,128)}, f32[2,32]{1,0:T(2,128)}) custom-call(f32[3,2048]{1,0:T(4,128)} %get-tuple-element.6.refs_0_, f32[3,2048]{1,0:T(4,128)} %get-tuple-element.7.refs_1_, f32[2,32]{1,0:T(2,128)} %get-tuple-element.8.refs_2_), custom_call_target="tpu_custom_call" | custom-call | tf_op jit(solution)/shard_map/pallas_call | solution.py:596

commit v4 on v3

--- a/solution.py
+++ b/solution.py
@@ -14,7 +14,6 @@
 NEAR_RATE = 0.5
 FAR = 1e30
 LANES = 128
-TERMS = 24
 OPERANDS = 14
 F32 = jnp.float32
 BF16 = jnp.bfloat16
@@ -50,6 +49,22 @@
 
 def silu_of_double(half):
     return half + half * jnp.tanh(half)
+
+
+def order_of_work(quads):
+    many = range(2 * quads)
+    order = [("project", u) for u in range(quads)] + [("read", u) for u in range(quads)]
+    order.append(("score", 0))
+    for k in many:
+        if k + 1 in many:
+            order.append(("score", k + 1))
+        order.append(("weigh", k))
+        if k - 2 in many:
+            order.append(("mix", k - 2))
+    order += [("mix", k) for k in many[-2:]]
+    order += [("flatten", k) for k in many]
+    order += [("pull", k) for k in many]
+    return order
 
 
 def kernel(tiles, slots, heads, *refs):
@@ -63,15 +78,13 @@
         rows,
         cols,
         counts,
-        spots,
+        places,
         own_rows,
         neigh_rows,
         projections,
         head_readout,
         pulls,
         atom_energy,
-        firsts,
-        seconds,
         load_sem,
         send_sem,
         recv_sem,
@@ -256,36 +269,42 @@
 
     quads = pairs // 2
     many = range(pairs)
-    nothing = jnp.zeros((2 * TERMS, LANES), BF16)
-
-    def set_distances(centred):
-        def parts(x):
-            high = x.astype(BF16).astype(F32)
-            middle = (x - high).astype(BF16).astype(F32)
-            return high, middle, x - high - middle
-
-        ones = jnp.ones((slots, LANES), F32)
-        terms = []
-        norm = None
-        for x in centred:
-            norm = x * x if norm is None else norm + x * x
-            h, m, l = parts(x)
-            terms += [(h, h), (h, m), (m, h), (h, l), (l, h), (m, m)]
-        terms = [(-2.0 * a, b) for a, b in terms]
-        for n in parts(norm):
-            terms += [(n, ones), (ones, n)]
-        for k, (a, b) in enumerate(terms):
-            firsts[:, k, :] = a[0:pairs]
-            firsts[:, TERMS + k, :] = a[pairs:]
-            seconds[:, k, :] = jnp.where(left_rows, b[0:pairs], 0.0)
-            seconds[:, TERMS + k, :] = jnp.where(left_rows, 0.0, b[pairs:])
+    nothing = jnp.zeros((48, LANES), BF16)
+
+    norm_row = jnp.bitwise_and(sub8, 3) == 0
+    own_lanes = (sub8 < 4) == left8
+
+    def set_places(centred):
+        norm = centred[0] * centred[0] + centred[1] * centred[1] + centred[2] * centred[2]
+        for c, values in enumerate([norm] + centred):
+            places[:, c, :] = values[0:pairs]
+            places[:, c + 4, :] = values[pairs:]
+
+    def distance_factors(pair):
+        place = places[pair]
+        high = place.astype(BF16).astype(F32)
+        middle = (place - high).astype(BF16).astype(F32)
+        low = place - high - middle
+        high_one = jnp.where(norm_row, 1.0, high)
+        left = [high, middle, low, high_one, jnp.where(norm_row, 1.0, middle), high_one]
+        once = jnp.where(norm_row, 1.0, -2.0 * high)
+        cross = -2.0 * middle
+        right = [
+            once,
+            once,
+            once,
+            jnp.where(norm_row, high, cross),
+            jnp.where(norm_row, middle, cross),
+            jnp.where(norm_row, low, -2.0 * low),
+        ]
+        right = [jnp.where(own_lanes, part, 0.0) for part in right]
+        return jnp.concatenate(left, axis=0), jnp.concatenate(right, axis=0).astype(BF16)
 
     def model():
         far, hidden = [], []
         for u in range(quads):
-            both = firsts[2 * u : 2 * u + 2].reshape(4 * TERMS, LANES)
-            left = jnp.transpose(both)[0:atoms].astype(BF16)
-            right = [seconds[2 * u + v].astype(BF16) for v in range(2)]
+            left, right = zip(distance_factors(2 * u), distance_factors(2 * u + 1))
+            left = jnp.transpose(jnp.concatenate(left, axis=0))[0:atoms].astype(BF16)
             right = jnp.concatenate(
                 [
                     jnp.concatenate([right[0], nothing], axis=0),
@@ -315,25 +334,29 @@
         for k in many:
             span = slice(k * LANES, (k + 1) * LANES)
             hidden.append(silu_of_double(summed[k] + own_rows[span, :]).astype(BF16))
-        query, key, value, base = [], [], [], []
-        for u in range(quads):
+        query, key, value, base, reads = {}, {}, {}, {}, {}
+        parts, weights, mixed, lefts = {}, {}, {}, {}
+
+        def project(u):
             block = jnp.concatenate(hidden[2 * u : 2 * u + 2], axis=0)
-            query.append(dot_nn(block, w_query[...]).astype(BF16))
+            query[u] = dot_nn(block, w_query[...]).astype(BF16)
             across = dot_nt(projections[...], block)
-            key.append(across[0:width].astype(BF16))
-            value.append(across[width : 2 * width].astype(BF16))
-            base.append(across[2 * width : 2 * width + 16] + across[2 * width + 16 :])
-        reads = [dot_nn(head_readout[...], value[u]) for u in range(quads)]
-        reads = [read[0 : 16 * heads] + read[16 * heads :] for read in reads]
-
-        def scores(k):
+            key[u] = across[0:width].astype(BF16)
+            value[u] = across[width : 2 * width].astype(BF16)
+            base[u] = across[2 * width : 2 * width + 16] + across[2 * width + 16 :]
+
+        def read(u):
+            product = dot_nn(head_readout[...], value[u])
+            reads[u] = product[0 : 16 * heads] + product[16 * heads :]
+
+        def score(k):
             u, span = k // 2, slice((k % 2) * LANES, (k % 2 + 1) * LANES)
             straight = key[u][:, span]
             turned = pltpu.roll(straight, atoms, 1)
             result = []
             for m in range(2):
                 at = (2 * (k % 2) + m) * atoms
-                parts = []
+                scored = []
                 for g in range(groups):
                     blocks = []
                     for h in range(per_group):
@@ -349,37 +372,29 @@
                                 axis=1,
                             )
                         )
-                    parts.append(
+                    scored.append(
                         dot_nn(
                             query[u][at : at + atoms, g * LANES : (g + 1) * LANES],
                             jnp.concatenate(blocks, axis=0),
                         )
                     )
-                result.append(parts)
-            return result
-
-        def weigh(k, parts):
+                result.append(scored)
+            parts[k] = result
+
+        def weigh(k):
             turned = pltpu.roll(far[k], atoms, 1)
             result = []
             for m in range(2):
                 here = jnp.where(left64, far[k], turned) if m == 0 else jnp.where(left64, turned, far[k])
                 tiles_out = []
                 for t in range(heads // 2):
-                    part = parts[m][t // 2][:, (t % 2) * LANES : (t % 2 + 1) * LANES]
+                    part = parts[k][m][t // 2][:, (t % 2) * LANES : (t % 2 + 1) * LANES]
                     envelope = jnp.exp(here * decay_rows[t])
                     tiles_out.append((silu_of_double(part * half_scale) * envelope).astype(BF16))
                 result.append(jnp.concatenate(tiles_out, axis=1))
-            return jnp.concatenate(result, axis=0)
-
-        weights = []
-        ahead_scores = scores(0)
-        for k in many:
-            now = ahead_scores
-            if k + 1 < pairs:
-                ahead_scores = scores(k + 1)
-            weights.append(weigh(k, now))
-        mixed = []
-        for k in many:
+            weights[k] = jnp.concatenate(result, axis=0)
+
+        def mix(k):
             u, span = k // 2, slice((k % 2) * LANES, (k % 2 + 1) * LANES)
             straight = reads[u][:, span]
             turned = pltpu.roll(straight, atoms, 1)
@@ -403,29 +418,39 @@
             left_hi = left.astype(BF16)
             left_lo = (left - left_hi.astype(F32)).astype(BF16)
             product = dot_nt(jnp.concatenate([left_hi, left_lo], axis=0), weights[k])
-            mixed.append(product[0:32] + product[32:64])
-        lefts = []
-        for k in many:
+            mixed[k] = product[0:32] + product[32:64]
+
+        def flatten(k):
             u, span = k // 2, slice((k % 2) * LANES, (k % 2 + 1) * LANES)
             scalars = jnp.where(left16, mixed[k][0:16], mixed[k][16:32]) + base[u][:, span]
             atom_energy[k : k + 1, :] = scalars[heads : heads + 1]
             straight = scalars[0:heads]
             turned = pltpu.roll(straight, atoms, 1)
+            place = places[k]
+            swapped = pltpu.roll(place, 4, 0)
             left = []
             for m in range(2):
                 a, b = (straight, turned) if m == 0 else (turned, straight)
                 here = jnp.where(left8, a, b)
-                place = spots[m * pairs + k]
+                a, b = (place, swapped) if m == 0 else (swapped, place)
+                spot = jnp.where(norm_row, 1.0, jnp.where(sub8 < 4, a, b))
                 terms = []
                 for t in range(heads // 2):
-                    term = jnp.sum(here * flat_masks[t], axis=0, keepdims=True) * place
+                    term = jnp.sum(here * flat_masks[t], axis=0, keepdims=True) * spot
                     term_hi = term.astype(BF16).astype(F32)
                     terms.append(jnp.where(sub8 < 4, term_hi, term - term_hi))
                 left.append(jnp.concatenate(terms, axis=1))
-            lefts.append(jnp.concatenate(left, axis=0).astype(BF16))
-        for k in many:
+            lefts[k] = jnp.concatenate(left, axis=0).astype(BF16)
+
+        def pull(k):
             pulled = dot_nt(lefts[k], weights[k])
             pulls[k] = jnp.where(left8, pulled[0:8], pulled[8:16])
+
+        steps = dict(
+            project=project, read=read, score=score, weigh=weigh, mix=mix, flatten=flatten, pull=pull
+        )
+        for name, k in order_of_work(quads):
+            steps[name](k)
 
     def finish_energy(step):
         each = atom_energy[...]
@@ -450,12 +475,8 @@
         centred = [field - field[:, 0:1] for field in fields[:3]]
         for c in range(3):
             rows[c] = jnp.where(left_rows, centred[c][0:pairs], centred[c][pairs:])
-            spots[:, c + 1, :] = centred[c]
-            spots[:, c + 5, :] = centred[c]
-        set_distances(centred)
+        set_places(centred)
         if step == 0:
-            spots[:, 0, :] = jnp.ones((slots, LANES), F32)
-            spots[:, 4, :] = jnp.ones((slots, LANES), F32)
             sort = jnp.where(half_lane.astype(F32) < count, fields[3], -1.0)
             cols[...] = jnp.transpose(jnp.concatenate([sort] * (LANES // slots), axis=0))[0:atoms]
             both_tables = jnp.concatenate([embed[...] * 0.5, neigh[...] * 0.5], axis=1).astype(BF16)
@@ -576,15 +597,13 @@
             pltpu.VMEM((3, slots // 2, LANES), F32),
             pltpu.VMEM((atoms, LANES), F32),
             pltpu.VMEM((slots // 2, LANES), F32),
-            pltpu.VMEM((slots, 8, LANES), F32),
+            pltpu.VMEM((slots // 2, 8, LANES), F32),
             pltpu.VMEM((slots * atoms, width), F32),
             pltpu.VMEM((slots * atoms, width), BF16),
             pltpu.VMEM((2 * width + 32, width), BF16),
             pltpu.VMEM((32 * heads, width), BF16),
             pltpu.VMEM((slots // 2, 8, LANES), F32),
             pltpu.VMEM((slots // 2, LANES), F32),
-            pltpu.VMEM((slots // 2, 2 * TERMS, LANES), F32),
-            pltpu.VMEM((slots // 2, 2 * TERMS, LANES), F32),
             pltpu.SemaphoreType.DMA((OPERANDS,)),
             pltpu.SemaphoreType.DMA((STEPS + 1, 2)),
             pltpu.SemaphoreType.DMA((STEPS + 1, 2)),

time: 37.3 us -> 35.8 us (0.960)
  Pallas kernels: 36.4 us -> 34.9 us
    pallas_call x1, Pallas kernels: 35 us -> 33.5 us  [body(): pl.pallas_call(functools.partial(kernel, tiles, slots, heads), out_shape=...]
where the time goes in v4:
time: 35.8 us; the launch traced here: 35.6 us
  Pallas kernels  34.9 us (97%)
  between operations  0.64 us (2%)
    pallas_call x1, Pallas kernels, body(): pl.pallas_call(functools.partial(kernel, tiles, slots, heads), out_shape=...  33.5 us
    pallas_call x1, Pallas kernels, body(): pl.pallas_call(hand_over, out_shape=tuple((jax.ShapeDtypeStruct(result.sh...  1.41 us

profile of v4, /device:TPU:56, one launch (start us, length us, event | category | flops | bytes accessed | tf_op | source)
XLA Modules:
  0.0 35.6 jit_solution(11965191046131590615)
XLA Ops:
  0.6 33.5 %shard_map.157 = (f32[3,2048]{1,0:T(4,128)}, f32[3,2048]{1,0:T(4,128)}, f32[2,32]{1,0:T(2,128)}) custom-call(f32[3,2048]{1,0:T(4,128)} %refs_0_.1, f32[3,2048]{1,0:T(4,128)} %refs_1_.1, f32[16,128]{1,0:T(8,128)} %bitcast.5, s32[16,128]{1,0:T(8,128)} %bitcast.6, s32[32,64]{1,0:T(8,128)} %refs_4_.1, s32[2,32]{1,0:T(2,128)} %refs_5_.1, ...), custom_call_target="tpu_custom_call" | custom-call | tf_op jit(solution)/shard_map/pallas_call | solution.py:583
  34.1 1.4 %shard_map.158 = (f32[3,2048]{1,0:T(4,128)}, f32[3,2048]{1,0:T(4,128)}, f32[2,32]{1,0:T(2,128)}) custom-call(f32[3,2048]{1,0:T(4,128)} %get-tuple-element.6.refs_0_, f32[3,2048]{1,0:T(4,128)} %get-tuple-element.7.refs_1_, f32[2,32]{1,0:T(2,128)} %get-tuple-element.8.refs_2_), custom_call_target="tpu_custom_call" | custom-call | tf_op jit(solution)/shard_map/pallas_call | solution.py:615

commit v5 on v4

--- a/solution.py
+++ b/solution.py
@@ -61,13 +61,26 @@
         order.append(("weigh", k))
         if k - 2 in many:
             order.append(("mix", k - 2))
+        if k - 4 in many:
+            order.append(("flatten", k - 4))
+        if k - 6 in many:
+            order.append(("pull", k - 6))
     order += [("mix", k) for k in many[-2:]]
-    order += [("flatten", k) for k in many]
-    order += [("pull", k) for k in many]
+    order += [("flatten", k) for k in many[-4:]]
+    order += [("pull", k) for k in many[-6:]]
     return order
 
 
 def kernel(tiles, slots, heads, *refs):
+    doms = lax.axis_size("dom")
+    me = lax.axis_index("dom")
+    upper, lower = lax.rem(me + 1, doms), lax.rem(me + doms - 1, doms)
+    barrier = pltpu.get_barrier_semaphore()
+    for neighbour in (lower, upper):
+        pl.semaphore_signal(
+            barrier, inc=1, device_id={"dom": neighbour}, device_id_type=pl.DeviceIdType.MESH
+        )
+
     operands, refs = refs[:OPERANDS], refs[OPERANDS:]
     (positions_out, velocities_out, energies_out), refs = refs[:3], refs[3:]
     local, refs = refs[:OPERANDS], refs[OPERANDS:]
@@ -111,19 +124,10 @@
         w_force,
         head_decay,
     ) = local
-    doms = lax.axis_size("dom")
-    me = lax.axis_index("dom")
-    upper, lower = lax.rem(me + 1, doms), lax.rem(me + doms - 1, doms)
     width = w_query.shape[0]
     head_width = width // heads
     ext_rows = ext.shape[1]
     types = embed.shape[0]
-
-    barrier = pltpu.get_barrier_semaphore()
-    for neighbour in (lower, upper):
-        pl.semaphore_signal(
-            barrier, inc=1, device_id={"dom": neighbour}, device_id_type=pl.DeviceIdType.MESH
-        )
 
     lane = iota((slots, LANES), 1)
 
@@ -234,9 +238,6 @@
     decay_rows = [
         -jnp.where(left8[0:1], head_decay[:, 2 * t : 2 * t + 1], head_decay[:, 2 * t + 1 : 2 * t + 2])
         for t in range(heads // 2)
-    ]
-    flat_masks = [
-        jnp.where(sub8 == 2 * t + jnp.where(left8, 0, 1), 1.0, 0.0) for t in range(heads // 2)
     ]
     empty = jnp.zeros((head_width, LANES), BF16)
 
@@ -430,13 +431,13 @@
             swapped = pltpu.roll(place, 4, 0)
             left = []
             for m in range(2):
-                a, b = (straight, turned) if m == 0 else (turned, straight)
-                here = jnp.where(left8, a, b)
+                low, high = (straight, turned) if m == 0 else (turned, straight)
                 a, b = (place, swapped) if m == 0 else (swapped, place)
                 spot = jnp.where(norm_row, 1.0, jnp.where(sub8 < 4, a, b))
                 terms = []
                 for t in range(heads // 2):
-                    term = jnp.sum(here * flat_masks[t], axis=0, keepdims=True) * spot
+                    flat = jnp.where(left8, low[2 * t : 2 * t + 1], high[2 * t + 1 : 2 * t + 2])
+                    term = flat * spot
                     term_hi = term.astype(BF16).astype(F32)
                     terms.append(jnp.where(sub8 < 4, term_hi, term - term_hi))
                 left.append(jnp.concatenate(terms, axis=1))

time: 35.8 us -> 35.5 us (level)
  no operation moved by 1% of the time
where the time goes in v5:
time: 35.5 us; the launch traced here: 35.3 us
  Pallas kernels  34.7 us (98%)
  between operations  0.64 us (2%)
    pallas_call x1, Pallas kernels, body(): pl.pallas_call(functools.partial(kernel, tiles, slots, heads), out_shape=...  33.3 us
    pallas_call x1, Pallas kernels, body(): pl.pallas_call(hand_over, out_shape=tuple((jax.ShapeDtypeStruct(result.sh...  1.41 us

profile of v5, /device:TPU:56, one launch (start us, length us, event | category | flops | bytes accessed | tf_op | source)
XLA Modules:
  0.0 35.3 jit_solution(13635438454479630950)
XLA Ops:
  0.6 33.3 %shard_map.157 = (f32[3,2048]{1,0:T(4,128)}, f32[3,2048]{1,0:T(4,128)}, f32[2,32]{1,0:T(2,128)}) custom-call(f32[3,2048]{1,0:T(4,128)} %refs_0_.1, f32[3,2048]{1,0:T(4,128)} %refs_1_.1, f32[16,128]{1,0:T(8,128)} %bitcast.5, s32[16,128]{1,0:T(8,128)} %bitcast.6, s32[32,64]{1,0:T(8,128)} %refs_4_.1, s32[2,32]{1,0:T(2,128)} %refs_5_.1, ...), custom_call_target="tpu_custom_call" | custom-call | tf_op jit(solution)/shard_map/pallas_call | solution.py:584
  33.9 1.4 %shard_map.158 = (f32[3,2048]{1,0:T(4,128)}, f32[3,2048]{1,0:T(4,128)}, f32[2,32]{1,0:T(2,128)}) custom-call(f32[3,2048]{1,0:T(4,128)} %get-tuple-element.6.refs_0_, f32[3,2048]{1,0:T(4,128)} %get-tuple-element.7.refs_1_, f32[2,32]{1,0:T(2,128)} %get-tuple-element.8.refs_2_), custom_call_target="tpu_custom_call" | custom-call | tf_op jit(solution)/shard_map/pallas_call | solution.py:616

commit v6 on v5

--- a/solution.py
+++ b/solution.py
@@ -316,7 +316,8 @@
             squared = dot_nn(left, right)
             for v in range(2):
                 inside = latest < counts[2 * u + v : 2 * u + v + 1, :]
-                far.append(jnp.where(inside, squared[:, v * LANES : (v + 1) * LANES], FAR))
+                apart = jnp.maximum(squared[:, v * LANES : (v + 1) * LANES], 0.0)
+                far.append(jnp.where(inside, jnp.where(distinct, apart, 0.0), FAR))
         summed = []
         for k in many:
             nearby = jnp.where(distinct, jnp.exp(-NEAR_RATE * far[k]), 0.0)

time: 35.5 us -> 35.7 us (level)
  no operation moved by 1% of the time
where the time goes in v6:
time: 35.7 us; the launch traced here: 35.4 us
  Pallas kernels  34.8 us (97%)
  between operations  0.64 us (2%)
    pallas_call x1, Pallas kernels, body(): pl.pallas_call(functools.partial(kernel, tiles, slots, heads), out_shape=...  33.4 us
    pallas_call x1, Pallas kernels, body(): pl.pallas_call(hand_over, out_shape=tuple((jax.ShapeDtypeStruct(result.sh...  1.41 us

profile of v6, /device:TPU:56, one launch (start us, length us, event | category | flops | bytes accessed | tf_op | source)
XLA Modules:
  0.0 35.4 jit_solution(11318151822599512554)
XLA Ops:
  0.6 33.4 %shard_map.157 = (f32[3,2048]{1,0:T(4,128)}, f32[3,2048]{1,0:T(4,128)}, f32[2,32]{1,0:T(2,128)}) custom-call(f32[3,2048]{1,0:T(4,128)} %refs_0_.1, f32[3,2048]{1,0:T(4,128)} %refs_1_.1, f32[16,128]{1,0:T(8,128)} %bitcast.5, s32[16,128]{1,0:T(8,128)} %bitcast.6, s32[32,64]{1,0:T(8,128)} %refs_4_.1, s32[2,32]{1,0:T(2,128)} %refs_5_.1, ...), custom_call_target="tpu_custom_call" | custom-call | tf_op jit(solution)/shard_map/pallas_call | solution.py:585
  34.0 1.4 %shard_map.158 = (f32[3,2048]{1,0:T(4,128)}, f32[3,2048]{1,0:T(4,128)}, f32[2,32]{1,0:T(2,128)}) custom-call(f32[3,2048]{1,0:T(4,128)} %get-tuple-element.6.refs_0_, f32[3,2048]{1,0:T(4,128)} %get-tuple-element.7.refs_1_, f32[2,32]{1,0:T(2,128)} %get-tuple-element.8.refs_2_), custom_call_target="tpu_custom_call" | custom-call | tf_op jit(solution)/shard_map/pallas_call | solution.py:617
